TPU v7x, 256 devices: a whole 4x4x8 slice. The times are simulated.
256 devices in a mesh: seq: 64 (over z_hi, x, y, core), tp: 4 (over z_lo).
Axes of the slice: x: 4, y: 4, z: 8 (z_hi: 2, z_lo: 4; z = z_hi * 4 + z_lo), core: 2. Of those that a mesh axis runs over, the one named last changes fastest.
Arguments:
- cotangent: bfloat16 [49152, 2048], P('seq', 'tp'), may hold values from -16 to 16
- gate_codes: bfloat16 [49152, 7168], P('seq', 'tp'), may hold values from -127 to 127, as said below
- up_codes: bfloat16 [49152, 7168], P('seq', 'tp'), may hold values from -127 to 127, as said below
- gate_scale: float32 [49152], P('seq'), may hold values from 0.004 to 0.04
- up_scale: float32 [49152], P('seq'), may hold values from 0.004 to 0.04
- down_weight: bfloat16 [2048, 7168], P('seq', 'tp'), may hold values from -0.125 to 0.125
Outputs:
- gate_grad: bfloat16 [49152, 7168], P('seq', 'tp')
- up_grad: bfloat16 [49152, 7168], P('seq', 'tp')
- weight_grad: float32 [2048, 7168], P('seq', 'tp')
Inputs may be any that keep to these rules, and one draw needn't show every extreme that they name: `gate_codes`: every entry is a whole number. `up_codes`: every entry is a whole number.
All inputs are finite; a program needn't handle non-finite values.
Results may differ from a plain program's by a relative error of at most 0.003.
Values may be sent and summed in bfloat16 or wider, within the bound.
No kernel may reach another device: no remote copies, remote signals or barrier semaphores. Data moves between devices by JAX's collectives and lax.ppermute only.
A program may use at most 128 MiB of HBM per device.

v0:
```python
import math

import jax
import jax.numpy as jnp
from jax import lax
from jax.sharding import PartitionSpec as P


def on_device(cotangent, gate_codes, up_codes, gate_scale, up_scale, down_weight):
    local_tokens = cotangent.shape[0]
    normalizer = 1.0 / math.sqrt(local_tokens * lax.axis_size("seq"))
    cotangent_all = lax.all_gather(cotangent, "tp", axis=1, tiled=True)
    gate_value = gate_codes.astype(jnp.float32) * gate_scale[:, None]
    up_value = up_codes.astype(jnp.float32) * up_scale[:, None]
    sigmoid_gate = jax.nn.sigmoid(gate_value)
    hidden_act = (gate_value * sigmoid_gate * up_value).astype(jnp.bfloat16)
    whole_weight = lax.all_gather(down_weight, "seq", axis=0, tiled=True)
    hidden_grad = jnp.dot(cotangent_all, whole_weight, preferred_element_type=jnp.float32)
    whole_term = lax.dot_general(
        cotangent_all, hidden_act, (((0,), (0,)), ((), ())), preferred_element_type=jnp.float32
    )
    weight_grad = lax.psum_scatter(whole_term * normalizer, "seq", scatter_dimension=0, tiled=True)
    gate_grad = (
        hidden_grad * up_value * sigmoid_gate * (1.0 + gate_value * (1.0 - sigmoid_gate))
    ).astype(jnp.bfloat16)
    up_grad = (hidden_grad * gate_value * sigmoid_gate).astype(jnp.bfloat16)
    return (gate_grad, up_grad, weight_grad)


def solution(mesh):
    placed = (P("seq", "tp"), P("seq", "tp"), P("seq", "tp"), P("seq"), P("seq"), P("seq", "tp"))
    return jax.shard_map(
        on_device,
        mesh=mesh,
        in_specs=placed,
        out_specs=(P("seq", "tp"), P("seq", "tp"), P("seq", "tp")),
        check_vma=False,
    )
```

profile of v0, /device:TPU:32, one launch (start us, length us, event | category | flops | bytes accessed | tf_op | source)
XLA Modules:
  0.0 631.4 jit_solution(13413322310064577257)
XLA Ops:
  7.2 0.0 all-gather.3.cloned.1.call-start
  7.2 0.7 all-gather.3.cloned.1.call-update
  7.9 0.0 all-gather.5.cloned.1.call-start
  7.9 0.7 all-gather.5.cloned.1.call-update
  8.6 0.0 reduce-scatter.4.cloned.1.call-start
  8.7 70.4 %all-gather.3.cloned.1.call-done = bf16[768,2048]{1,0:T(8,128)(2,1)} async-done(((bf16[768,512]{1,0:T(8,128)(2,1)}), bf16[768,2048]{1,0:T(8,128)(2,1)}) %all-gather.3.cloned.1.call-update) | async-done | bytes 3145744 | tf_op jit(solution)/shard_map/all_gather | solution.py:12
  79.1 12.8 %multiply_bitcast_fusion = f32[2048,1792]{0,1:T(8,128)} fusion(bf16[768,2048]{1,0:T(8,128)(2,1)} %all-gather.3.cloned.1.call-done, bf16[768,1792]{1,0:T(8,128)(2,1)} %param.7, bf16[768,1792]{1,0:T(8,128)(2,1)} %param.8, f32[768]{0:T(1024)} %param.9, f32[768]{0:T(1024)} %param.10), kind=kOutput, calls=%fused_computation | convolution fusion | flops 5654577152 | bytes 23336960 | tf_op jit(solution)/shard_map/dot_general | solution.py:19
  91.9 14.3 %copy.11 = f32[2048,1792]{1,0:T(8,128)} copy(f32[2048,1792]{0,1:T(8,128)} %multiply_bitcast_fusion) | data formatting | bytes 29360128
  106.2 0.0 copy-start
  106.2 0.0 copy-start.1
  106.2 0.0 copy-start.2
  106.2 0.0 reduce-scatter.4.cloned.1.call-update
  106.2 83.9 %all-gather.5.cloned.1.call-done = bf16[2048,1792]{1,0:T(8,128)(2,1)} async-done(((bf16[32,1792]{1,0:T(8,128)(2,1)}), bf16[2048,1792]{1,0:T(8,128)(2,1)}) %all-gather.5.cloned.1.call-update) | async-done | bytes 7340048 | tf_op jit(solution)/shard_map/all_gather | solution.py:17
  190.1 0.0 copy-done
  190.1 0.0 copy-done.1
  190.1 0.0 copy-done.2
  190.1 13.0 %multiply_convert_fusion.1 = (bf16[768,1792]{1,0:T(8,128)(2,1)}, bf16[768,1792]{1,0:T(8,128)(2,1)}) fusion(bf16[768,1792]{1,0:T(8,128)(2,1)} %param.7, f32[768]{0:T(1024)S(1)} %copy-done.1, f32[768]{0:T(1024)S(1)} %copy-done.2, bf16[768,1792]{1,0:T(8,128)(2,1)} %param.8, bf16[768,2048]{1,0:T(8,128)(2,1)S(1)} %copy-done, ...), kind=kOutput, calls=%fused_computation.2 | convolution fusion | flops 5660540928 | bytes 21501952 | tf_op jit(solution)/shard_map/dot_general | solution.py:18
  203.2 421.7 %reduce-scatter.4.cloned.1.call-done = f32[32,1792]{1,0:T(8,128)} async-done(((f32[2048,1792]{1,0:T(8,128)}), f32[32,1792]{1,0:T(8,128)}) %reduce-scatter.4.cloned.1.call-update) | async-done | bytes 229392
Async XLA Ops:
  7.2 72.0 %all-gather.3.cloned.1.call-start = ((), (), s32[]{:S(2)}) async-start(), calls=%async_computation.1 | async-start | bytes 3932160 | tf_op jit(solution)/shard_map/all_gather | solution.py:12
  7.9 182.2 %all-gather.5.cloned.1.call-start = ((), (), s32[]{:S(2)}) async-start(), calls=%async_computation.2 | async-start | bytes 7454720 | tf_op jit(solution)/shard_map/all_gather | solution.py:17
  8.6 616.2 %reduce-scatter.4.cloned.1.call-start = ((), (), s32[]{:S(2)}) async-start(), calls=%async_computation.3 | async-start | bytes 14909440
  106.2 84.0 %copy-start = (bf16[768,2048]{1,0:T(8,128)(2,1)S(1)}, bf16[768,2048]{1,0:T(8,128)(2,1)}, u32[]{:S(2)}) copy-start(bf16[768,2048]{1,0:T(8,128)(2,1)} %all-gather.3.cloned.1.call-done) | copy-start | bytes 9437188
  106.2 84.0 %copy-start.1 = (f32[768]{0:T(1024)S(1)}, f32[768]{0:T(1024)}, u32[]{:S(2)}) copy-start(f32[768]{0:T(1024)} %param.9) | copy-start | bytes 9220
  106.2 84.0 %copy-start.2 = (f32[768]{0:T(1024)S(1)}, f32[768]{0:T(1024)}, u32[]{:S(2)}) copy-start(f32[768]{0:T(1024)} %param.10) | copy-start | bytes 9220
Sparse Core Ops, SparseCore 0:
  9.8 69.2 all-gather.2
  82.7 107.4 all-gather.4
  193.3 431.4 reduce-scatter.3
where the time goes:
time: 632 us; the launch traced here: 631 us
  waiting for transfers between devices  577 us (91%)
  matrix products  25.8 us (4%)
  local copies, waits for them, and re-layouts  14.3 us (2%)
  between operations  13.7 us (2%)
    unnamed x4, waiting for transfers between devices  423 us
    all_gather x1, waiting for transfers between devices, on_device(): whole_weight = lax.all_gather(down_weight, 'seq', axis=0, tiled=True)  83.9 us
    all_gather x1, waiting for transfers between devices, on_device(): cotangent_all = lax.all_gather(cotangent, 'tp', axis=1, tiled=True)  70.4 us
    unnamed x7, local copies, waits for them, and re-layouts  14.3 us
    dot_general x1, matrix products, on_device(): jnp.dot(cotangent_all, whole_weight, preferred_element_type=jnp.float32)  13 us
    dot_general x1, matrix products, on_device(): lax.dot_general(cotangent_all, hidden_act, (((0,), (0,)), ((), ())), pref...  12.8 us
  transfers between devices with their start and end apart: 3, of which 3 were waited for; matrix products, arithmetic and copies ran while one was open for 6% of the time, Pallas kernels for 0%

commit v1 on v0

v1 whole, which is shorter than its diff:
```python
import math

import jax
import jax.numpy as jnp
from jax import lax
from jax.experimental import pallas as pl
from jax.experimental.pallas import tpu as pltpu
from jax.sharding import Mesh, PartitionSpec as P

SEQ = ("zh", "x", "y", "c")
BF, F32 = jnp.bfloat16, jnp.float32
BLOCK = 128
VMEM = 58 << 20


def shift(n, k):
    return [(i, (i + k) % n) for i in range(n)]


def flip(n, m):
    return [(i, i ^ m) for i in range(n)]


def after(value, *events):
    return lax.optimization_barrier((value, events))[0]


def cost(seconds):
    return pl.CostEstimate(flops=int(seconds * 1e15), bytes_accessed=0, transcendentals=0)


def column(row):
    return jnp.broadcast_to(row, (8, BLOCK)).T[:, :1]


def gates(gate_codes, up_codes, gate_scale, up_scale):
    g = gate_codes[...].astype(F32) * column(gate_scale[0])
    u = up_codes[...].astype(F32) * column(up_scale[0])
    return g, u, jax.nn.sigmoid(g)


def hidden_kernel(gate_codes, up_codes, gate_scale, up_scale, out):
    g, u, s = gates(gate_codes, up_codes, gate_scale, up_scale)
    out[...] = (g * s * u).astype(BF)


def hidden_of(gate_codes, up_codes, gate_scale, up_scale):
    tokens, cols = gate_codes.shape
    rows = pl.BlockSpec((BLOCK, cols), lambda i: (i, 0))
    scale = pl.BlockSpec((1, 1, BLOCK), lambda i: (i, 0, 0))
    return pl.pallas_call(
        hidden_kernel,
        grid=(tokens // BLOCK,),
        in_specs=[rows, rows, scale, scale],
        out_specs=rows,
        out_shape=jax.ShapeDtypeStruct((tokens, cols), BF),
        compiler_params=pltpu.CompilerParams(vmem_limit_bytes=VMEM),
        cost_estimate=cost(50e-6),
    )(gate_codes, up_codes, gate_scale, up_scale)


def grads_kernel(places, *refs):
    slots, others, weight = refs[:4], refs[4:8], refs[8]
    gate_codes, up_codes, gate_scale, up_scale = refs[9:13]
    gate_out, up_out, whole, sems = refs[-4:]

    def part(k, c):
        return pltpu.make_async_copy(weight.at[places[k], :, places[4 + c]], whole.at[k, c], sems.at[k, c])

    parts = [(k, c) for k in range(4) for c in range(2)]

    @pl.when(pl.program_id(0) == 0)
    def _():
        for k, c in parts:
            part(k, c).start()

    grad = None
    for k, c in parts:
        pl.when(pl.program_id(0) == 0)(part(k, c).wait)
        rows = (slots, others)[c][k][...].T
        term = jnp.dot(rows, whole[k, c].reshape(256, -1), preferred_element_type=F32)
        grad = term if grad is None else grad + term
    g, u, s = gates(gate_codes, up_codes, gate_scale, up_scale)
    gate_out[...] = (grad * u * s * (1.0 + g * (1.0 - s))).astype(BF)
    up_out[...] = (grad * g * s).astype(BF)


def grads_of(places, slots, others, weight, codes):
    tokens, cols = codes[0].shape
    rows = pl.BlockSpec((BLOCK, cols), lambda i, _: (i, 0))
    scale = pl.BlockSpec((1, 1, BLOCK), lambda i, _: (i, 0, 0))
    slot = pl.BlockSpec((256, BLOCK), lambda i, _: (0, i))
    out = jax.ShapeDtypeStruct((tokens, cols), BF)
    given = (places, *slots, *others, weight, *codes)
    return pl.pallas_call(
        grads_kernel,
        grid_spec=pltpu.PrefetchScalarGridSpec(
            num_scalar_prefetch=1,
            grid=(tokens // BLOCK,),
            in_specs=[slot] * 8
            + [pl.BlockSpec(memory_space=pltpu.HBM)]
            + [rows, rows, scale, scale],
            out_specs=[rows, rows],
            scratch_shapes=[pltpu.VMEM((4, 2, 8, 32, cols), BF), pltpu.SemaphoreType.DMA((4, 2))],
        ),
        out_shape=[out, out],
        compiler_params=pltpu.CompilerParams(vmem_limit_bytes=VMEM),
        cost_estimate=cost(50e-6),
    )(*given)


def owner_of_first(x, t):
    return (t - (t + x // 2) % 2) % 4 // 2


def on_device(cot, gate_codes, up_codes, gate_scale, up_scale, weight):
    zh, x, y, c, t = (lax.axis_index(n) for n in ("zh", "x", "y", "c", "t"))
    tokens, cols = gate_codes.shape
    normalizer = 1.0 / math.sqrt(tokens * 64)
    codes = (gate_codes, up_codes, gate_scale.reshape(-1, 1, BLOCK), up_scale.reshape(-1, 1, BLOCK))

    bar = lax.optimization_barrier

    def for_grads(slot):
        return over_core(slot[:, tokens:])

    def ring(slot):
        return lax.ppermute(slot, "t", shift(4, 1))

    def over_core(block):
        return lax.ppermute(block, "c", shift(2, 1))

    def over_y(near, far, opposite):
        return [lax.ppermute(b, "y", shift(4, d)) for d, b in ((1, near), (3, far), (2, opposite))]

    def summed(own, got):
        for block in got:
            own = own + block.astype(F32)
        return own

    def products(slot):
        total = jnp.dot(slot[:, :tokens], mine, preferred_element_type=F32)
        total += jnp.dot(slot[:, tokens:], other, preferred_element_type=F32)
        total = total.reshape(2, 4, 32, cols)
        block = lambda d: lax.dynamic_index_in_dim(total, (y + d) % 4, 1, keepdims=False)
        return block(0), block(1).astype(BF), block(3).astype(BF), block(2).astype(BF)

    def at_x(even, odd):
        def rows(m):
            to = x ^ m
            block = lambda a: lax.dynamic_index_in_dim(a, to % 2, 0, keepdims=False)
            return jnp.where(t % 2 == to // 2, block(even), block(odd))

        return rows

    def over_x(places, rows):
        return [lax.ppermute(rows(m).astype(BF), "x", flip(4, m)) for m in places]

    a = cot.T.reshape(2, 4, 2, 32, tokens).transpose(2, 0, 1, 3, 4).reshape(2, 256, tokens)
    kept, sent = lax.optimization_barrier((jnp.where(c == 0, a[0], a[1]), jnp.where(c == 0, a[1], a[0])))
    peer = lax.ppermute(after(weight, sent), "zh", shift(2, 1))
    mine = hidden_of(*codes)
    slot0, mine, peer = bar((jnp.concatenate([kept, over_core(sent)], axis=1), mine, peer))
    held = jnp.where(zh == 0, jnp.stack([weight, peer]), jnp.stack([peer, weight]))
    whole = lax.all_gather(held, ("x", "y", "c"), axis=1, tiled=True)

    slot1 = ring(slot0)
    other = over_core(mine)
    other0 = for_grads(slot0)
    p0 = products(slot0)
    slot1, other, other0, p0, slot0 = bar((slot1, other, other0, p0, slot0))

    slot2 = ring(slot1)
    y0 = over_y(*p0[1:])
    other1 = for_grads(slot1)
    p1 = products(slot1)
    slot2, y0, other1, p1, slot1 = bar((slot2, y0, other1, p1, slot1))

    slot3 = ring(slot2)
    y1 = over_y(*p1[1:])
    other2 = for_grads(slot2)
    p2 = products(slot2)
    slot3, y1, other2, p2, slot2 = bar((slot3, y1, other2, p2, slot2))

    y0, y1 = bar((summed(p0[0], y0), summed(p1[0], y1)))
    y2 = over_y(*p2[1:])
    x01 = over_x((1,), at_x(y0, y1))
    other3 = for_grads(slot3)
    p3 = products(slot3)
    y2, x01, p3, slot3, other3, whole = bar((y2, x01, p3, slot3, other3, whole))

    places = jnp.stack([(t - k) % 4 for k in range(4)] + [c, 1 - c]).astype(jnp.int32)
    slots = (slot0, slot1, slot2, slot3)
    others = (other0, other1, other2, other3)
    y3 = over_y(*p3[1:])
    x01 += over_x((3, 2), at_x(y0, y1))
    grads = grads_of(places, slots, others, whole.reshape(4, 8, 2, 32, cols), codes)
    y2 = summed(p2[0], y2)
    y2, y3, x01, grads = bar((y2, y3, x01, grads))

    y3 = summed(p3[0], y3)
    x23 = over_x((1, 3, 2), at_x(y2, y3))
    first = summed(at_x(y0, y1)(0), x01)
    x23, first = bar((x23, first))
    second = summed(at_x(y2, y3)(0), x23)

    here = owner_of_first(x, t) == zh
    got = lax.ppermute(jnp.where(here, second, first).astype(BF), "zh", shift(2, 1))
    weight_grad = (jnp.where(here, first, second) + got.astype(F32)) * normalizer
    return grads[0], grads[1], weight_grad


def solution(mesh):
    fine = Mesh(mesh.devices.reshape(2, 4, 4, 2, 4), SEQ + ("t",))
    both, rows = P(SEQ, "t"), P(SEQ)
    return jax.shard_map(
        on_device,
        mesh=fine,
        in_specs=(both, both, both, rows, rows, both),
        out_specs=(both, both, both),
        check_vma=False,
    )
```

time: 632 us -> 154 us (0.24)
  waiting for transfers between devices: 577 us -> 53.7 us
  starting transfers between devices: 0.11 us -> 42.7 us
  Pallas kernels: 0 us -> 25.6 us
  matrix products: 25.8 us -> 7.09 us
  local copies, waits for them, and re-layouts: 14.3 us -> 4.64 us
    unnamed x4 -> x1, waiting for transfers between devices: 423 us -> 0.02 us
    all_gather x2 -> x1, waiting for transfers between devices: 154 us -> 0.02 us  [on_device(): whole = lax.all_gather(held, ('x', 'y', 'c'), axis=1, tiled=True)]
    ppermute x0 -> x29, waiting for transfers between devices: none -> 53.7 us  [the longest x12 23.1 us: over_y(): lax.ppermute(b, 'y', shift(4, d))]
    ppermute x0 -> x29, starting transfers between devices: none -> 42.6 us  [the longest x12 17.4 us: over_y(): lax.ppermute(b, 'y', shift(4, d))]
    pallas_call x0 -> x2, Pallas kernels: none -> 25.6 us  [the longest x1 19.1 us: grads_of(): pl.pallas_call(grads_kernel, grid_spec=pltpu.PrefetchScalarGridSpec(num_s...]
    dot_general x2 -> x8, matrix products: 25.8 us -> 7.09 us  [the longest x4 3.56 us: products(): total = jnp.dot(slot[:, :tokens], mine, preferred_element_type=F32)]
    unnamed x7 -> x29, local copies, waits for them, and re-layouts: 14.3 us -> 1.47 us
  transfers between devices with their start and end apart: 3 -> 30, of which waited for: 3 -> 15; matrix products, arithmetic and copies ran while one was open for 6% -> 8% of each run, Pallas kernels for 0% -> 17%
where the time goes in v1:
time: 154 us; the launch traced here: 153 us
  waiting for transfers between devices  53.7 us (35%)
  starting transfers between devices  42.7 us (28%)
  Pallas kernels  25.6 us (17%)
  between operations  14.7 us (10%)
  matrix products  7.09 us (5%)
  local copies, waits for them, and re-layouts  4.64 us (3%)
  other arithmetic  4.19 us (3%)
    ppermute x12, waiting for transfers between devices, over_y(): lax.ppermute(b, 'y', shift(4, d))  23.1 us
    pallas_call x1, Pallas kernels, grads_of(): pl.pallas_call(grads_kernel, grid_spec=pltpu.PrefetchScalarGridSpec(num_s...  19.1 us
    ppermute x3, waiting for transfers between devices, ring(): return lax.ppermute(slot, 't', shift(4, 1))  18 us
    ppermute x12, starting transfers between devices, over_y(): lax.ppermute(b, 'y', shift(4, d))  17.4 us
    ppermute x6, starting transfers between devices, over_x(): return [lax.ppermute(rows(m).astype(BF), 'x', flip(4, m)) for m in places]  11.3 us
    pallas_call x1, Pallas kernels, hidden_of(): pl.pallas_call(hidden_kernel, grid=(tokens // BLOCK,), in_specs=[rows, ro...  6.49 us
    ppermute x1, starting transfers between devices, on_device(): peer = lax.ppermute(after(weight, sent), 'zh', shift(2, 1))  6.38 us
    ppermute x6, waiting for transfers between devices, over_x(): return [lax.ppermute(rows(m).astype(BF), 'x', flip(4, m)) for m in places]  5.48 us
  transfers between devices with their start and end apart: 30, of which 15 were waited for; matrix products, arithmetic and copies ran while one was open for 8% of the time, Pallas kernels for 17%

profile of v1, /device:TPU:32, one launch (start us, length us, event | category | flops | bytes accessed | tf_op | source)
XLA Modules:
  0.0 152.6 jit_solution(9552245886291387574)
XLA Ops:
  8.8 6.4 %collective-permute-start.1 = (bf16[32,1792]{1,0:T(8,128)(2,1)S(1)}, bf16[32,1792]{1,0:T(8,128)(2,1)S(1)}, u32[]{:S(2)}, u32[]{:S(2)}) collective-permute-start(bf16[32,1792]{1,0:T(8,128)(2,1)S(1)} %copy-done.8), channel_id=1, source_target_pairs={{0,128},{128,0},{1,129},{129,1},{2,130},{130,2},{3,131},{131,3},{4... | collective-permute-start | bytes 344072 | tf_op jit(solution)/shard_map/ppermute | solution.py:161
  16.4 6.5 %shard_map.85 = bf16[768,1792]{1,0:T(8,128)(2,1)} custom-call(bf16[768,1792]{1,0:T(8,128)(2,1)} %refs_9_.1, bf16[768,1792]{1,0:T(8,128)(2,1)} %refs_10_.1, f32[6,1,128]{2,1,0:T(1,128)} %reshape.74.gate_scale.refs_11_, f32[6,1,128]{2,1,0:T(1,128)} %reshape.75.up_scale.refs_12_), custom_call_target="tpu_custom_call" | custom-call | flops 49999998976 | tf_op jit(solution)/shard_map/pallas_call | solution.py:51
  26.0 3.2 %collective-permute-done.3 = bf16[768,1792]{1,0:T(8,128)(2,1)S(1)} collective-permute-done((bf16[768,1792]{1,0:T(8,128)(2,1)}, bf16[768,1792]{1,0:T(8,128)(2,1)S(1)}, u32[]{:S(2)}, u32[]{:S(2)}) %collective-permute-start.3) | collective-permute-done | bytes 2752544 | tf_op jit(solution)/shard_map/ppermute | solution.py:131
  31.2 13.3 %collective-permute-done.2.refs_1_ = bf16[256,1536]{1,0:T(8,128)(2,1)S(1)} collective-permute-done((bf16[256,1536]{1,0:T(8,128)(2,1)S(1)}, bf16[256,1536]{1,0:T(8,128)(2,1)S(1)}, u32[]{:S(2)}, u32[]{:S(2)}) %collective-permute-start.2) | collective-permute-done | bytes 786464 | tf_op jit(solution)/shard_map/ppermute | solution.py:128
  47.2 1.7 %collective-permute-start.7 = (bf16[2,32,1792]{2,1,0:T(8,128)(2,1)S(1)}, bf16[2,32,1792]{2,1,0:T(8,128)(2,1)S(1)}, u32[]{:S(2)}, u32[]{:S(2)}) collective-permute-start(bf16[2,32,1792]{2,1,0:T(8,128)(2,1)S(1)} %get-tuple-element.72), channel_id=1, source_target_pairs={{0,24},{8,0},{16,8},{24,16},{1,25},{9,1},{17,9},{25,17},{2,26},{10... | collective-permute-start | bytes 688136 | tf_op jit(solution)/shard_map/ppermute | solution.py:134
  48.9 2.0 %collective-permute-start.8 = (bf16[2,32,1792]{2,1,0:T(8,128)(2,1)S(1)}, bf16[2,32,1792]{2,1,0:T(8,128)(2,1)S(1)}, u32[]{:S(2)}, u32[]{:S(2)}) collective-permute-start(bf16[2,32,1792]{2,1,0:T(8,128)(2,1)S(1)} %get-tuple-element.73), channel_id=1, source_target_pairs={{0,16},{8,24},{16,0},{24,8},{1,17},{9,25},{17,1},{25,9},{2,18},{10... | collective-permute-start | bytes 688136 | tf_op jit(solution)/shard_map/ppermute | solution.py:134
  52.8 2.2 %collective-permute-done.6 = bf16[2,32,1792]{2,1,0:T(8,128)(2,1)S(1)} collective-permute-done((bf16[2,32,1792]{2,1,0:T(8,128)(2,1)S(1)}, bf16[2,32,1792]{2,1,0:T(8,128)(2,1)S(1)}, u32[]{:S(2)}, u32[]{:S(2)}) %collective-permute-start.6) | collective-permute-done | bytes 229408 | tf_op jit(solution)/shard_map/ppermute | solution.py:134
  55.0 2.9 %collective-permute-done.7 = bf16[2,32,1792]{2,1,0:T(8,128)(2,1)S(1)} collective-permute-done((bf16[2,32,1792]{2,1,0:T(8,128)(2,1)S(1)}, bf16[2,32,1792]{2,1,0:T(8,128)(2,1)S(1)}, u32[]{:S(2)}, u32[]{:S(2)}) %collective-permute-start.7) | collective-permute-done | bytes 229408 | tf_op jit(solution)/shard_map/ppermute | solution.py:134
  57.8 1.8 %collective-permute-done.8 = bf16[2,32,1792]{2,1,0:T(8,128)(2,1)S(1)} collective-permute-done((bf16[2,32,1792]{2,1,0:T(8,128)(2,1)S(1)}, bf16[2,32,1792]{2,1,0:T(8,128)(2,1)S(1)}, u32[]{:S(2)}, u32[]{:S(2)}) %collective-permute-start.8) | collective-permute-done | bytes 229408 | tf_op jit(solution)/shard_map/ppermute | solution.py:134
  59.6 4.7 %collective-permute-done.5.refs_2_ = bf16[256,1536]{1,0:T(8,128)(2,1)S(1)} collective-permute-done((bf16[256,1536]{1,0:T(8,128)(2,1)S(1)}, bf16[256,1536]{1,0:T(8,128)(2,1)S(1)}, u32[]{:S(2)}, u32[]{:S(2)}) %collective-permute-start.5) | collective-permute-done | bytes 786464 | tf_op jit(solution)/shard_map/ppermute | solution.py:128
  64.4 1.8 %collective-permute-start.11 = (bf16[2,32,1792]{2,1,0:T(8,128)(2,1)S(1)}, bf16[2,32,1792]{2,1,0:T(8,128)(2,1)S(1)}, u32[]{:S(2)}, u32[]{:S(2)}) collective-permute-start(bf16[2,32,1792]{2,1,0:T(8,128)(2,1)S(1)} %get-tuple-element.76), channel_id=1, source_target_pairs={{0,8},{8,16},{16,24},{24,0},{1,9},{9,17},{17,25},{25,1},{2,10},{10... | collective-permute-start | bytes 688136 | tf_op jit(solution)/shard_map/ppermute | solution.py:134
  67.9 2.0 %collective-permute-start.13 = (bf16[2,32,1792]{2,1,0:T(8,128)(2,1)S(1)}, bf16[2,32,1792]{2,1,0:T(8,128)(2,1)S(1)}, u32[]{:S(2)}, u32[]{:S(2)}) collective-permute-start(bf16[2,32,1792]{2,1,0:T(8,128)(2,1)S(1)} %get-tuple-element.78), channel_id=1, source_target_pairs={{0,16},{8,24},{16,0},{24,8},{1,17},{9,25},{17,1},{25,9},{2,18},{10... | collective-permute-start | bytes 688136 | tf_op jit(solution)/shard_map/ppermute | solution.py:134
  72.7 6.1 %collective-permute-done.11 = bf16[2,32,1792]{2,1,0:T(8,128)(2,1)S(1)} collective-permute-done((bf16[2,32,1792]{2,1,0:T(8,128)(2,1)S(1)}, bf16[2,32,1792]{2,1,0:T(8,128)(2,1)S(1)}, u32[]{:S(2)}, u32[]{:S(2)}) %collective-permute-start.11) | collective-permute-done | bytes 229408 | tf_op jit(solution)/shard_map/ppermute | solution.py:134
  79.6 8.0 %collective-permute-done.13 = bf16[2,32,1792]{2,1,0:T(8,128)(2,1)S(1)} collective-permute-done((bf16[2,32,1792]{2,1,0:T(8,128)(2,1)S(1)}, bf16[2,32,1792]{2,1,0:T(8,128)(2,1)S(1)}, u32[]{:S(2)}, u32[]{:S(2)}) %collective-permute-start.13) | collective-permute-done | bytes 229408 | tf_op jit(solution)/shard_map/ppermute | solution.py:134
  88.3 2.6 %collective-permute-start.16 = (bf16[2,32,1792]{2,1,0:T(8,128)(2,1)S(1)}, bf16[2,32,1792]{2,1,0:T(8,128)(2,1)}, u32[]{:S(2)}, u32[]{:S(2)}) collective-permute-start(bf16[2,32,1792]{2,1,0:T(8,128)(2,1)S(1)} %get-tuple-element.81), channel_id=1, source_target_pairs={{0,24},{8,0},{16,8},{24,16},{1,25},{9,1},{17,9},{25,17},{2,26},{10... | collective-permute-start | bytes 688136 | tf_op jit(solution)/shard_map/ppermute | solution.py:134
  96.7 2.7 %collective-permute-start.23 = (bf16[32,1792]{1,0:T(8,128)(2,1)}, bf16[32,1792]{1,0:T(8,128)(2,1)S(1)}, u32[]{:S(2)}, u32[]{:S(2)}) collective-permute-start(bf16[32,1792]{1,0:T(8,128)(2,1)} %get-tuple-element.145), channel_id=1, source_target_pairs={{0,96},{32,64},{64,32},{96,0},{1,97},{33,65},{65,33},{97,1},{2,98}... | collective-permute-start | bytes 344072 | tf_op jit(solution)/shard_map/ppermute | solution.py:157
  100.7 3.0 %collective-permute-start.24 = (bf16[32,1792]{1,0:T(8,128)(2,1)}, bf16[32,1792]{1,0:T(8,128)(2,1)S(1)}, u32[]{:S(2)}, u32[]{:S(2)}) collective-permute-start(bf16[32,1792]{1,0:T(8,128)(2,1)} %get-tuple-element.144), channel_id=1, source_target_pairs={{0,64},{32,96},{64,0},{96,32},{1,65},{33,97},{65,1},{97,33},{2,66}... | collective-permute-start | bytes 344072 | tf_op jit(solution)/shard_map/ppermute | solution.py:157
  103.8 3.2 %collective-permute-start.21 = (bf16[2,32,1792]{2,1,0:T(8,128)(2,1)S(1)}, bf16[2,32,1792]{2,1,0:T(8,128)(2,1)S(1)}, u32[]{:S(2)}, u32[]{:S(2)}) collective-permute-start(bf16[2,32,1792]{2,1,0:T(8,128)(2,1)S(1)} %get-tuple-element.99), channel_id=1, source_target_pairs={{0,24},{8,0},{16,8},{24,16},{1,25},{9,1},{17,9},{25,17},{2,26},{10... | collective-permute-start | bytes 688136 | tf_op jit(solution)/shard_map/ppermute | solution.py:134
  107.1 19.1 %shard_map.86 = (bf16[768,1792]{1,0:T(8,128)(2,1)}, bf16[768,1792]{1,0:T(8,128)(2,1)}) custom-call(s32[6]{0:T(128)} %stack.45.places, bf16[256,1536]{1,0:T(8,128)(2,1)} %copy-done.1, bf16[256,1536]{1,0:T(8,128)(2,1)} %copy-done.5, bf16[256,1536]{1,0:T(8,128)(2,1)} %copy-done.6, bf16[256,1536]{1,0:T(8,128)(2,1)} %copy-done.7, bf16[256,768]{1,0:T(8,128)(2,1)} %copy-done.11, ...), custom_call_target="tpu_custom_call" | custom-call | flops 49999998976 | tf_op jit(solution)/shard_map/pallas_call | solution.py:95
  129.8 2.0 %collective-permute-start.27 = (bf16[32,1792]{1,0:T(8,128)(2,1)S(1)}, bf16[32,1792]{1,0:T(8,128)(2,1)S(1)}, u32[]{:S(2)}, u32[]{:S(2)}) collective-permute-start(bf16[32,1792]{1,0:T(8,128)(2,1)S(1)} %get-tuple-element.141), channel_id=1, source_target_pairs={{0,64},{32,96},{64,0},{96,32},{1,65},{33,97},{65,1},{97,33},{2,66}... | collective-permute-start | bytes 344072 | tf_op jit(solution)/shard_map/ppermute | solution.py:157
  132.5 1.8 %collective-permute-done.26 = bf16[32,1792]{1,0:T(8,128)(2,1)S(1)} collective-permute-done((bf16[32,1792]{1,0:T(8,128)(2,1)S(1)}, bf16[32,1792]{1,0:T(8,128)(2,1)S(1)}, u32[]{:S(2)}, u32[]{:S(2)}) %collective-permute-start.26) | collective-permute-done | bytes 114720 | tf_op jit(solution)/shard_map/ppermute | solution.py:157
  134.3 1.8 %collective-permute-done.27 = bf16[32,1792]{1,0:T(8,128)(2,1)S(1)} collective-permute-done((bf16[32,1792]{1,0:T(8,128)(2,1)S(1)}, bf16[32,1792]{1,0:T(8,128)(2,1)S(1)}, u32[]{:S(2)}, u32[]{:S(2)}) %collective-permute-start.27) | collective-permute-done | bytes 114720 | tf_op jit(solution)/shard_map/ppermute | solution.py:157
  136.2 4.9 %collective-permute-start.28 = (bf16[32,1792]{1,0:T(8,128)(2,1)S(1)}, bf16[32,1792]{1,0:T(8,128)(2,1)S(1)}, u32[]{:S(2)}, u32[]{:S(2)}) collective-permute-start(bf16[32,1792]{1,0:T(8,128)(2,1)S(1)} %get-tuple-element.127), channel_id=1, source_target_pairs={{0,128},{128,0},{1,129},{129,1},{2,130},{130,2},{3,131},{131,3},{4... | collective-permute-start | bytes 344072 | tf_op jit(solution)/shard_map/ppermute | solution.py:208
  141.1 4.0 %collective-permute-done.28 = bf16[32,1792]{1,0:T(8,128)(2,1)S(1)} collective-permute-done((bf16[32,1792]{1,0:T(8,128)(2,1)S(1)}, bf16[32,1792]{1,0:T(8,128)(2,1)S(1)}, u32[]{:S(2)}, u32[]{:S(2)}) %collective-permute-start.28) | collective-permute-done | bytes 114720 | tf_op jit(solution)/shard_map/ppermute | solution.py:208
  (103 shorter events, 30.3 us)
Async XLA Ops:
  7.2 96.5 %all-gather.2.cloned.1.call-start = ((), (), s32[]{:S(2)}) async-start(), calls=%async_computation | async-start | bytes 7569408 | tf_op jit(solution)/shard_map/all_gather | solution.py:165
  8.7 14.2 %collective-permute-start = (bf16[256,768]{1,0:T(8,128)(2,1)S(1)}, bf16[256,768]{1,0:T(8,128)(2,1)S(1)}, u32[]{:S(2)}, u32[]{:S(2)}) collective-permute-start(bf16[256,768]{1,0:T(8,128)(2,1)S(1)} %bitcast.143), channel_id=1, source_target_pairs={{0,4},{4,0},{1,5},{5,1},{2,6},{6,2},{3,7},{7,3},{8,12},{12,8},{9,1... | collective-permute-start | bytes 1179656 | tf_op jit(solution)/shard_map/ppermute | solution.py:131
  8.8 14.1 %collective-permute-start.1 = (bf16[32,1792]{1,0:T(8,128)(2,1)S(1)}, bf16[32,1792]{1,0:T(8,128)(2,1)S(1)}, u32[]{:S(2)}, u32[]{:S(2)}) collective-permute-start(bf16[32,1792]{1,0:T(8,128)(2,1)S(1)} %copy-done.8), channel_id=1, source_target_pairs={{0,128},{128,0},{1,129},{129,1},{2,130},{130,2},{3,131},{131,3},{4... | collective-permute-start | bytes 344072 | tf_op jit(solution)/shard_map/ppermute | solution.py:161
  24.9 19.6 %collective-permute-start.2 = (bf16[256,1536]{1,0:T(8,128)(2,1)S(1)}, bf16[256,1536]{1,0:T(8,128)(2,1)S(1)}, u32[]{:S(2)}, u32[]{:S(2)}) collective-permute-start(bf16[256,1536]{1,0:T(8,128)(2,1)S(1)} %pad_maximum_fusion.refs_0_), channel_id=1, source_target_pairs={{0,1},{1,2},{2,3},{3,0},{4,5},{5,6},{6,7},{7,4},{8,9},{9,10},{10,1... | collective-permute-start | bytes 2359304 | tf_op jit(solution)/shard_map/ppermute | solution.py:128
  44.5 19.8 %collective-permute-start.5 = (bf16[256,1536]{1,0:T(8,128)(2,1)S(1)}, bf16[256,1536]{1,0:T(8,128)(2,1)S(1)}, u32[]{:S(2)}, u32[]{:S(2)}) collective-permute-start(bf16[256,1536]{1,0:T(8,128)(2,1)S(1)} %collective-permute-done.2.refs_1_), channel_id=1, source_target_pairs={{0,1},{1,2},{2,3},{3,0},{4,5},{5,6},{6,7},{7,4},{8,9},{9,10},{10,1... | collective-permute-start | bytes 2359304 | tf_op jit(solution)/shard_map/ppermute | solution.py:128
  45.5 9.4 %collective-permute-start.6 = (bf16[2,32,1792]{2,1,0:T(8,128)(2,1)S(1)}, bf16[2,32,1792]{2,1,0:T(8,128)(2,1)S(1)}, u32[]{:S(2)}, u32[]{:S(2)}) collective-permute-start(bf16[2,32,1792]{2,1,0:T(8,128)(2,1)S(1)} %get-tuple-element.71), channel_id=1, source_target_pairs={{0,8},{8,16},{16,24},{24,0},{1,9},{9,17},{17,25},{25,1},{2,10},{10... | collective-permute-start | bytes 688136 | tf_op jit(solution)/shard_map/ppermute | solution.py:134
  47.2 10.6 %collective-permute-start.7 = (bf16[2,32,1792]{2,1,0:T(8,128)(2,1)S(1)}, bf16[2,32,1792]{2,1,0:T(8,128)(2,1)S(1)}, u32[]{:S(2)}, u32[]{:S(2)}) collective-permute-start(bf16[2,32,1792]{2,1,0:T(8,128)(2,1)S(1)} %get-tuple-element.72), channel_id=1, source_target_pairs={{0,24},{8,0},{16,8},{24,16},{1,25},{9,1},{17,9},{25,17},{2,26},{10... | collective-permute-start | bytes 688136 | tf_op jit(solution)/shard_map/ppermute | solution.py:134
  48.9 10.8 %collective-permute-start.8 = (bf16[2,32,1792]{2,1,0:T(8,128)(2,1)S(1)}, bf16[2,32,1792]{2,1,0:T(8,128)(2,1)S(1)}, u32[]{:S(2)}, u32[]{:S(2)}) collective-permute-start(bf16[2,32,1792]{2,1,0:T(8,128)(2,1)S(1)} %get-tuple-element.73), channel_id=1, source_target_pairs={{0,16},{8,24},{16,0},{24,8},{1,17},{9,25},{17,1},{25,9},{2,18},{10... | collective-permute-start | bytes 688136 | tf_op jit(solution)/shard_map/ppermute | solution.py:134
  50.8 8.8 %collective-permute-start.9 = (bf16[256,768]{1,0:T(8,128)(2,1)S(1)}, bf16[256,768]{1,0:T(8,128)(2,1)S(1)}, u32[]{:S(2)}, u32[]{:S(2)}) collective-permute-start(bf16[256,768]{1,0:T(8,128)(2,1)S(1)} %slice.42), channel_id=1, source_target_pairs={{0,4},{4,0},{1,5},{5,1},{2,6},{6,2},{3,7},{7,3},{8,12},{12,8},{9,1... | collective-permute-start | bytes 1179656 | tf_op jit(solution)/shard_map/ppermute | solution.py:131
  64.3 23.3 %collective-permute-start.10 = (bf16[256,1536]{1,0:T(8,128)(2,1)S(1)}, bf16[256,1536]{1,0:T(8,128)(2,1)S(1)}, u32[]{:S(2)}, u32[]{:S(2)}) collective-permute-start(bf16[256,1536]{1,0:T(8,128)(2,1)S(1)} %collective-permute-done.5.refs_2_), channel_id=1, source_target_pairs={{0,1},{1,2},{2,3},{3,0},{4,5},{5,6},{6,7},{7,4},{8,9},{9,10},{10,1... | collective-permute-start | bytes 2359304 | tf_op jit(solution)/shard_map/ppermute | solution.py:128
  64.4 14.4 %collective-permute-start.11 = (bf16[2,32,1792]{2,1,0:T(8,128)(2,1)S(1)}, bf16[2,32,1792]{2,1,0:T(8,128)(2,1)S(1)}, u32[]{:S(2)}, u32[]{:S(2)}) collective-permute-start(bf16[2,32,1792]{2,1,0:T(8,128)(2,1)S(1)} %get-tuple-element.76), channel_id=1, source_target_pairs={{0,8},{8,16},{16,24},{24,0},{1,9},{9,17},{17,25},{25,1},{2,10},{10... | collective-permute-start | bytes 688136 | tf_op jit(solution)/shard_map/ppermute | solution.py:134
  66.2 13.3 %collective-permute-start.12 = (bf16[2,32,1792]{2,1,0:T(8,128)(2,1)S(1)}, bf16[2,32,1792]{2,1,0:T(8,128)(2,1)S(1)}, u32[]{:S(2)}, u32[]{:S(2)}) collective-permute-start(bf16[2,32,1792]{2,1,0:T(8,128)(2,1)S(1)} %get-tuple-element.77), channel_id=1, source_target_pairs={{0,24},{8,0},{16,8},{24,16},{1,25},{9,1},{17,9},{25,17},{2,26},{10... | collective-permute-start | bytes 688136 | tf_op jit(solution)/shard_map/ppermute | solution.py:134
  67.9 19.7 %collective-permute-start.13 = (bf16[2,32,1792]{2,1,0:T(8,128)(2,1)S(1)}, bf16[2,32,1792]{2,1,0:T(8,128)(2,1)S(1)}, u32[]{:S(2)}, u32[]{:S(2)}) collective-permute-start(bf16[2,32,1792]{2,1,0:T(8,128)(2,1)S(1)} %get-tuple-element.78), channel_id=1, source_target_pairs={{0,16},{8,24},{16,0},{24,8},{1,17},{9,25},{17,1},{25,9},{2,18},{10... | collective-permute-start | bytes 688136 | tf_op jit(solution)/shard_map/ppermute | solution.py:134
  69.9 17.7 %collective-permute-start.14 = (bf16[256,768]{1,0:T(8,128)(2,1)S(1)}, bf16[256,768]{1,0:T(8,128)(2,1)S(1)}, u32[]{:S(2)}, u32[]{:S(2)}) collective-permute-start(bf16[256,768]{1,0:T(8,128)(2,1)S(1)} %slice.44), channel_id=1, source_target_pairs={{0,4},{4,0},{1,5},{5,1},{2,6},{6,2},{3,7},{7,3},{8,12},{12,8},{9,1... | collective-permute-start | bytes 1179656 | tf_op jit(solution)/shard_map/ppermute | solution.py:131
  87.6 13.1 %collective-permute-start.15 = (bf16[2,32,1792]{2,1,0:T(8,128)(2,1)S(1)}, bf16[2,32,1792]{2,1,0:T(8,128)(2,1)S(1)}, u32[]{:S(2)}, u32[]{:S(2)}) collective-permute-start(bf16[2,32,1792]{2,1,0:T(8,128)(2,1)S(1)} %get-tuple-element.80), channel_id=1, source_target_pairs={{0,8},{8,16},{16,24},{24,0},{1,9},{9,17},{17,25},{25,1},{2,10},{10... | collective-permute-start | bytes 688136 | tf_op jit(solution)/shard_map/ppermute | solution.py:134
  88.3 15.4 %collective-permute-start.16 = (bf16[2,32,1792]{2,1,0:T(8,128)(2,1)S(1)}, bf16[2,32,1792]{2,1,0:T(8,128)(2,1)}, u32[]{:S(2)}, u32[]{:S(2)}) collective-permute-start(bf16[2,32,1792]{2,1,0:T(8,128)(2,1)S(1)} %get-tuple-element.81), channel_id=1, source_target_pairs={{0,24},{8,0},{16,8},{24,16},{1,25},{9,1},{17,9},{25,17},{2,26},{10... | collective-permute-start | bytes 688136 | tf_op jit(solution)/shard_map/ppermute | solution.py:134
  90.9 12.8 %collective-permute-start.17 = (bf16[2,32,1792]{2,1,0:T(8,128)(2,1)S(1)}, bf16[2,32,1792]{2,1,0:T(8,128)(2,1)}, u32[]{:S(2)}, u32[]{:S(2)}) collective-permute-start(bf16[2,32,1792]{2,1,0:T(8,128)(2,1)S(1)} %get-tuple-element.82), channel_id=1, source_target_pairs={{0,16},{8,24},{16,0},{24,8},{1,17},{9,25},{17,1},{25,9},{2,18},{10... | collective-permute-start | bytes 688136 | tf_op jit(solution)/shard_map/ppermute | solution.py:134
  93.4 10.3 %collective-permute-start.19 = (bf16[256,768]{1,0:T(8,128)(2,1)S(1)}, bf16[256,768]{1,0:T(8,128)(2,1)}, u32[]{:S(2)}, u32[]{:S(2)}) collective-permute-start(bf16[256,768]{1,0:T(8,128)(2,1)S(1)} %slice.47), channel_id=1, source_target_pairs={{0,4},{4,0},{1,5},{5,1},{2,6},{6,2},{3,7},{7,3},{8,12},{12,8},{9,1... | collective-permute-start | bytes 1179656 | tf_op jit(solution)/shard_map/ppermute | solution.py:131
  96.7 30.7 %collective-permute-start.23 = (bf16[32,1792]{1,0:T(8,128)(2,1)}, bf16[32,1792]{1,0:T(8,128)(2,1)S(1)}, u32[]{:S(2)}, u32[]{:S(2)}) collective-permute-start(bf16[32,1792]{1,0:T(8,128)(2,1)} %get-tuple-element.145), channel_id=1, source_target_pairs={{0,96},{32,64},{64,32},{96,0},{1,97},{33,65},{65,33},{97,1},{2,98}... | collective-permute-start | bytes 344072 | tf_op jit(solution)/shard_map/ppermute | solution.py:157
  100.7 26.6 %collective-permute-start.24 = (bf16[32,1792]{1,0:T(8,128)(2,1)}, bf16[32,1792]{1,0:T(8,128)(2,1)S(1)}, u32[]{:S(2)}, u32[]{:S(2)}) collective-permute-start(bf16[32,1792]{1,0:T(8,128)(2,1)} %get-tuple-element.144), channel_id=1, source_target_pairs={{0,64},{32,96},{64,0},{96,32},{1,65},{33,97},{65,1},{97,33},{2,66}... | collective-permute-start | bytes 344072 | tf_op jit(solution)/shard_map/ppermute | solution.py:157
  103.7 23.6 %collective-permute-start.20 = (bf16[2,32,1792]{2,1,0:T(8,128)(2,1)S(1)}, bf16[2,32,1792]{2,1,0:T(8,128)(2,1)S(1)}, u32[]{:S(2)}, u32[]{:S(2)}) collective-permute-start(bf16[2,32,1792]{2,1,0:T(8,128)(2,1)S(1)} %get-tuple-element.98), channel_id=1, source_target_pairs={{0,8},{8,16},{16,24},{24,0},{1,9},{9,17},{17,25},{25,1},{2,10},{10... | collective-permute-start | bytes 688136 | tf_op jit(solution)/shard_map/ppermute | solution.py:134
  103.8 23.6 %collective-permute-start.21 = (bf16[2,32,1792]{2,1,0:T(8,128)(2,1)S(1)}, bf16[2,32,1792]{2,1,0:T(8,128)(2,1)S(1)}, u32[]{:S(2)}, u32[]{:S(2)}) collective-permute-start(bf16[2,32,1792]{2,1,0:T(8,128)(2,1)S(1)} %get-tuple-element.99), channel_id=1, source_target_pairs={{0,24},{8,0},{16,8},{24,16},{1,25},{9,1},{17,9},{25,17},{2,26},{10... | collective-permute-start | bytes 688136 | tf_op jit(solution)/shard_map/ppermute | solution.py:134
  107.1 20.3 %collective-permute-start.22 = (bf16[2,32,1792]{2,1,0:T(8,128)(2,1)S(1)}, bf16[2,32,1792]{2,1,0:T(8,128)(2,1)S(1)}, u32[]{:S(2)}, u32[]{:S(2)}) collective-permute-start(bf16[2,32,1792]{2,1,0:T(8,128)(2,1)S(1)} %get-tuple-element.100), channel_id=1, source_target_pairs={{0,16},{8,24},{16,0},{24,8},{1,17},{9,25},{17,1},{25,9},{2,18},{10... | collective-permute-start | bytes 688136 | tf_op jit(solution)/shard_map/ppermute | solution.py:134
  136.2 8.9 %collective-permute-start.28 = (bf16[32,1792]{1,0:T(8,128)(2,1)S(1)}, bf16[32,1792]{1,0:T(8,128)(2,1)S(1)}, u32[]{:S(2)}, u32[]{:S(2)}) collective-permute-start(bf16[32,1792]{1,0:T(8,128)(2,1)S(1)} %get-tuple-element.127), channel_id=1, source_target_pairs={{0,128},{128,0},{1,129},{129,1},{2,130},{130,2},{3,131},{131,3},{4... | collective-permute-start | bytes 344072 | tf_op jit(solution)/shard_map/ppermute | solution.py:208
  (20 other events, 141.2 us)
Sparse Core Ops, SparseCore 0:
  24.0 63.6 all-gather.1

commit v2 on v1

--- a/solution.py
+++ b/solution.py
@@ -10,6 +10,7 @@
 SEQ = ("zh", "x", "y", "c")
 BF, F32 = jnp.bfloat16, jnp.float32
 BLOCK = 128
+WIDE = 256
 VMEM = 58 << 20
 
 
@@ -33,24 +34,21 @@
     return jnp.broadcast_to(row, (8, BLOCK)).T[:, :1]
 
 
-def gates(gate_codes, up_codes, gate_scale, up_scale):
-    g = gate_codes[...].astype(F32) * column(gate_scale[0])
-    u = up_codes[...].astype(F32) * column(up_scale[0])
-    return g, u, jax.nn.sigmoid(g)
-
-
 def hidden_kernel(gate_codes, up_codes, gate_scale, up_scale, out):
-    g, u, s = gates(gate_codes, up_codes, gate_scale, up_scale)
-    out[...] = (g * s * u).astype(BF)
+    for i in range(gate_scale.shape[0]):
+        rows = slice(i * BLOCK, (i + 1) * BLOCK)
+        g = gate_codes[rows, :].astype(F32) * column(gate_scale[i])
+        u = up_codes[rows, :].astype(F32) * column(up_scale[i])
+        out[rows, :] = (g * jax.nn.sigmoid(g) * u).astype(BF)
 
 
 def hidden_of(gate_codes, up_codes, gate_scale, up_scale):
     tokens, cols = gate_codes.shape
-    rows = pl.BlockSpec((BLOCK, cols), lambda i: (i, 0))
-    scale = pl.BlockSpec((1, 1, BLOCK), lambda i: (i, 0, 0))
+    rows = pl.BlockSpec((tokens // 2, cols), lambda i: (i, 0))
+    scale = pl.BlockSpec((tokens // 2 // BLOCK, 1, BLOCK), lambda i: (i, 0, 0))
     return pl.pallas_call(
         hidden_kernel,
-        grid=(tokens // BLOCK,),
+        grid=(2,),
         in_specs=[rows, rows, scale, scale],
         out_specs=rows,
         out_shape=jax.ShapeDtypeStruct((tokens, cols), BF),
@@ -62,51 +60,52 @@
 def grads_kernel(places, *refs):
     slots, others, weight = refs[:4], refs[4:8], refs[8]
     gate_codes, up_codes, gate_scale, up_scale = refs[9:13]
-    gate_out, up_out, whole, sems = refs[-4:]
-
-    def part(k, c):
-        return pltpu.make_async_copy(weight.at[places[k], :, places[4 + c]], whole.at[k, c], sems.at[k, c])
-
-    parts = [(k, c) for k in range(4) for c in range(2)]
+    gate_out, up_out, rows, scales = refs[-4:]
+    tokens = gate_out.shape[0]
 
     @pl.when(pl.program_id(0) == 0)
     def _():
-        for k, c in parts:
-            part(k, c).start()
+        for k in range(4):
+            rows[k, 0] = slots[k][...].T
+            rows[k, 1] = others[k][...].T
+        for i in range(tokens // BLOCK):
+            for j, scale in enumerate((gate_scale, up_scale)):
+                scales[j, i * BLOCK : (i + 1) * BLOCK, :] = column(scale[i])
 
     grad = None
-    for k, c in parts:
-        pl.when(pl.program_id(0) == 0)(part(k, c).wait)
-        rows = (slots, others)[c][k][...].T
-        term = jnp.dot(rows, whole[k, c].reshape(256, -1), preferred_element_type=F32)
-        grad = term if grad is None else grad + term
-    g, u, s = gates(gate_codes, up_codes, gate_scale, up_scale)
+    for k in range(4):
+        for c in range(2):
+            part = weight[places[k], :, places[4 + c]].reshape(256, -1)
+            term = jnp.dot(rows[k, c], part, preferred_element_type=F32)
+            grad = term if grad is None else grad + term
+    g = gate_codes[...].astype(F32) * scales[0]
+    u = up_codes[...].astype(F32) * scales[1]
+    s = jax.nn.sigmoid(g)
     gate_out[...] = (grad * u * s * (1.0 + g * (1.0 - s))).astype(BF)
     up_out[...] = (grad * g * s).astype(BF)
 
 
 def grads_of(places, slots, others, weight, codes):
     tokens, cols = codes[0].shape
-    rows = pl.BlockSpec((BLOCK, cols), lambda i, _: (i, 0))
-    scale = pl.BlockSpec((1, 1, BLOCK), lambda i, _: (i, 0, 0))
-    slot = pl.BlockSpec((256, BLOCK), lambda i, _: (0, i))
+    block = pl.BlockSpec((tokens, WIDE), lambda i, _: (0, i))
+    once = lambda *shape: pl.BlockSpec(shape, lambda i, _: (0,) * len(shape), pipeline_mode=pl.Buffered(1))
     out = jax.ShapeDtypeStruct((tokens, cols), BF)
-    given = (places, *slots, *others, weight, *codes)
     return pl.pallas_call(
         grads_kernel,
         grid_spec=pltpu.PrefetchScalarGridSpec(
             num_scalar_prefetch=1,
-            grid=(tokens // BLOCK,),
-            in_specs=[slot] * 8
-            + [pl.BlockSpec(memory_space=pltpu.HBM)]
-            + [rows, rows, scale, scale],
-            out_specs=[rows, rows],
-            scratch_shapes=[pltpu.VMEM((4, 2, 8, 32, cols), BF), pltpu.SemaphoreType.DMA((4, 2))],
+            grid=(cols // WIDE,),
+            in_specs=[once(256, tokens)] * 8
+            + [pl.BlockSpec((4, 8, 2, 32, WIDE), lambda i, _: (0, 0, 0, 0, i))]
+            + [block, block]
+            + [once(*a.shape) for a in codes[2:]],
+            out_specs=[block, block],
+            scratch_shapes=[pltpu.VMEM((4, 2, tokens, 256), BF), pltpu.VMEM((2, tokens, 1), F32)],
         ),
         out_shape=[out, out],
         compiler_params=pltpu.CompilerParams(vmem_limit_bytes=VMEM),
         cost_estimate=cost(50e-6),
-    )(*given)
+    )(places, *slots, *others, weight, *codes)
 
 
 def owner_of_first(x, t):
@@ -187,9 +186,9 @@
     x01 = over_x((1,), at_x(y0, y1))
     other3 = for_grads(slot3)
     p3 = products(slot3)
-    y2, x01, p3, slot3, other3, whole = bar((y2, x01, p3, slot3, other3, whole))
-
-    places = jnp.stack([(t - k) % 4 for k in range(4)] + [c, 1 - c]).astype(jnp.int32)
+    y2, x01, p3, slot3, other3, whole, tt, cc = bar((y2, x01, p3, slot3, other3, whole, t, c))
+
+    places = jnp.stack([(tt - k) % 4 for k in range(4)] + [cc, 1 - cc]).astype(jnp.int32)
     slots = (slot0, slot1, slot2, slot3)
     others = (other0, other1, other2, other3)
     y3 = over_y(*p3[1:])

time: 154 us -> 150 us (0.974)
  Pallas kernels: 25.6 us -> 19.7 us
    pallas_call x1, Pallas kernels: 19.1 us -> 14.9 us  [grads_of(): pl.pallas_call(grads_kernel, grid_spec=pltpu.PrefetchScalarGridSpec(num_s...]
    ppermute x3, waiting for transfers between devices: 18 us -> 16 us  [ring(): return lax.ppermute(slot, 't', shift(4, 1))]
    pallas_call x1, Pallas kernels: 6.49 us -> 4.81 us  [hidden_of(): pl.pallas_call(hidden_kernel, grid=(2,), in_specs=[rows, rows, scale, sca...]
  transfers between devices with their start and end apart: 30 -> 30, of which waited for: 15 -> 15; matrix products, arithmetic and copies ran while one was open for 8% -> 8% of each run, Pallas kernels for 17% -> 13%
where the time goes in v2:
time: 150 us; the launch traced here: 149 us
  waiting for transfers between devices  54.7 us (36%)
  starting transfers between devices  43.8 us (29%)
  Pallas kernels  19.7 us (13%)
  between operations  14.8 us (10%)
  matrix products  7.09 us (5%)
  local copies, waits for them, and re-layouts  4.66 us (3%)
  other arithmetic  4.18 us (3%)
    ppermute x12, waiting for transfers between devices, over_y(): lax.ppermute(b, 'y', shift(4, d))  24.5 us
    ppermute x12, starting transfers between devices, over_y(): lax.ppermute(b, 'y', shift(4, d))  17.5 us
    ppermute x3, waiting for transfers between devices, ring(): return lax.ppermute(slot, 't', shift(4, 1))  16 us
    pallas_call x1, Pallas kernels, grads_of(): pl.pallas_call(grads_kernel, grid_spec=pltpu.PrefetchScalarGridSpec(num_s...  14.9 us
    ppermute x6, starting transfers between devices, over_x(): return [lax.ppermute(rows(m).astype(BF), 'x', flip(4, m)) for m in places]  11.3 us
    ppermute x6, waiting for transfers between devices, over_x(): return [lax.ppermute(rows(m).astype(BF), 'x', flip(4, m)) for m in places]  6.78 us
    ppermute x1, starting transfers between devices, on_device(): peer = lax.ppermute(after(weight, sent), 'zh', shift(2, 1))  6.38 us
    ppermute x1, starting transfers between devices, on_device(): lax.ppermute(jnp.where(here, second, first).astype(BF), 'zh', shift(2, 1))  5.19 us
  transfers between devices with their start and end apart: 30, of which 15 were waited for; matrix products, arithmetic and copies ran while one was open for 8% of the time, Pallas kernels for 13%

profile of v2, /device:TPU:32, one launch (start us, length us, event | category | flops | bytes accessed | tf_op | source)
XLA Modules:
  0.0 148.9 jit_solution(11597309206946399804)
XLA Ops:
  8.8 6.4 %collective-permute-start.1 = (bf16[32,1792]{1,0:T(8,128)(2,1)S(1)}, bf16[32,1792]{1,0:T(8,128)(2,1)S(1)}, u32[]{:S(2)}, u32[]{:S(2)}) collective-permute-start(bf16[32,1792]{1,0:T(8,128)(2,1)S(1)} %copy-done.8), channel_id=1, source_target_pairs={{0,128},{128,0},{1,129},{129,1},{2,130},{130,2},{3,131},{131,3},{4... | collective-permute-start | bytes 344072 | tf_op jit(solution)/shard_map/ppermute | solution.py:160
  16.4 4.8 %shard_map.85 = bf16[768,1792]{1,0:T(8,128)(2,1)} custom-call(bf16[768,1792]{1,0:T(8,128)(2,1)} %refs_9_.1, bf16[768,1792]{1,0:T(8,128)(2,1)} %refs_10_.1, f32[6,1,128]{2,1,0:T(1,128)} %reshape.74.gate_scale.refs_11_, f32[6,1,128]{2,1,0:T(1,128)} %reshape.75.up_scale.refs_12_), custom_call_target="tpu_custom_call" | custom-call | flops 49999998976 | tf_op jit(solution)/shard_map/pallas_call | solution.py:49
  24.1 3.6 %collective-permute-done.3 = bf16[768,1792]{1,0:T(8,128)(2,1)S(1)} collective-permute-done((bf16[768,1792]{1,0:T(8,128)(2,1)}, bf16[768,1792]{1,0:T(8,128)(2,1)S(1)}, u32[]{:S(2)}, u32[]{:S(2)}) %collective-permute-start.3) | collective-permute-done | bytes 2752544 | tf_op jit(solution)/shard_map/ppermute | solution.py:130
  29.6 12.7 %collective-permute-done.2.refs_1_ = bf16[256,1536]{1,0:T(8,128)(2,1)S(1)} collective-permute-done((bf16[256,1536]{1,0:T(8,128)(2,1)S(1)}, bf16[256,1536]{1,0:T(8,128)(2,1)S(1)}, u32[]{:S(2)}, u32[]{:S(2)}) %collective-permute-start.2) | collective-permute-done | bytes 786464 | tf_op jit(solution)/shard_map/ppermute | solution.py:127
  43.6 1.7 %collective-permute-start.6 = (bf16[2,32,1792]{2,1,0:T(8,128)(2,1)S(1)}, bf16[2,32,1792]{2,1,0:T(8,128)(2,1)S(1)}, u32[]{:S(2)}, u32[]{:S(2)}) collective-permute-start(bf16[2,32,1792]{2,1,0:T(8,128)(2,1)S(1)} %get-tuple-element.73), channel_id=1, source_target_pairs={{0,8},{8,16},{16,24},{24,0},{1,9},{9,17},{17,25},{25,1},{2,10},{10... | collective-permute-start | bytes 688136 | tf_op jit(solution)/shard_map/ppermute | solution.py:133
  45.3 1.6 %collective-permute-start.7 = (bf16[2,32,1792]{2,1,0:T(8,128)(2,1)S(1)}, bf16[2,32,1792]{2,1,0:T(8,128)(2,1)S(1)}, u32[]{:S(2)}, u32[]{:S(2)}) collective-permute-start(bf16[2,32,1792]{2,1,0:T(8,128)(2,1)S(1)} %get-tuple-element.74), channel_id=1, source_target_pairs={{0,24},{8,0},{16,8},{24,16},{1,25},{9,1},{17,9},{25,17},{2,26},{10... | collective-permute-start | bytes 688136 | tf_op jit(solution)/shard_map/ppermute | solution.py:133
  46.9 2.1 %collective-permute-start.8 = (bf16[2,32,1792]{2,1,0:T(8,128)(2,1)S(1)}, bf16[2,32,1792]{2,1,0:T(8,128)(2,1)S(1)}, u32[]{:S(2)}, u32[]{:S(2)}) collective-permute-start(bf16[2,32,1792]{2,1,0:T(8,128)(2,1)S(1)} %get-tuple-element.75), channel_id=1, source_target_pairs={{0,16},{8,24},{16,0},{24,8},{1,17},{9,25},{17,1},{25,9},{2,18},{10... | collective-permute-start | bytes 688136 | tf_op jit(solution)/shard_map/ppermute | solution.py:133
  50.9 1.8 %collective-permute-done.6 = bf16[2,32,1792]{2,1,0:T(8,128)(2,1)S(1)} collective-permute-done((bf16[2,32,1792]{2,1,0:T(8,128)(2,1)S(1)}, bf16[2,32,1792]{2,1,0:T(8,128)(2,1)S(1)}, u32[]{:S(2)}, u32[]{:S(2)}) %collective-permute-start.6) | collective-permute-done | bytes 229408 | tf_op jit(solution)/shard_map/ppermute | solution.py:133
  53.7 4.9 %collective-permute-done.8 = bf16[2,32,1792]{2,1,0:T(8,128)(2,1)S(1)} collective-permute-done((bf16[2,32,1792]{2,1,0:T(8,128)(2,1)S(1)}, bf16[2,32,1792]{2,1,0:T(8,128)(2,1)S(1)}, u32[]{:S(2)}, u32[]{:S(2)}) %collective-permute-start.8) | collective-permute-done | bytes 229408 | tf_op jit(solution)/shard_map/ppermute | solution.py:133
  58.7 3.3 %collective-permute-done.5.refs_2_ = bf16[256,1536]{1,0:T(8,128)(2,1)S(1)} collective-permute-done((bf16[256,1536]{1,0:T(8,128)(2,1)S(1)}, bf16[256,1536]{1,0:T(8,128)(2,1)S(1)}, u32[]{:S(2)}, u32[]{:S(2)}) %collective-permute-start.5) | collective-permute-done | bytes 786464 | tf_op jit(solution)/shard_map/ppermute | solution.py:127
  62.4 1.7 %collective-permute-start.11 = (bf16[2,32,1792]{2,1,0:T(8,128)(2,1)S(1)}, bf16[2,32,1792]{2,1,0:T(8,128)(2,1)S(1)}, u32[]{:S(2)}, u32[]{:S(2)}) collective-permute-start(bf16[2,32,1792]{2,1,0:T(8,128)(2,1)S(1)} %get-tuple-element.78), channel_id=1, source_target_pairs={{0,8},{8,16},{16,24},{24,0},{1,9},{9,17},{17,25},{25,1},{2,10},{10... | collective-permute-start | bytes 688136 | tf_op jit(solution)/shard_map/ppermute | solution.py:133
  65.8 2.1 %collective-permute-start.13 = (bf16[2,32,1792]{2,1,0:T(8,128)(2,1)S(1)}, bf16[2,32,1792]{2,1,0:T(8,128)(2,1)S(1)}, u32[]{:S(2)}, u32[]{:S(2)}) collective-permute-start(bf16[2,32,1792]{2,1,0:T(8,128)(2,1)S(1)} %get-tuple-element.80), channel_id=1, source_target_pairs={{0,16},{8,24},{16,0},{24,8},{1,17},{9,25},{17,1},{25,9},{2,18},{10... | collective-permute-start | bytes 688136 | tf_op jit(solution)/shard_map/ppermute | solution.py:133
  70.7 6.0 %collective-permute-done.11 = bf16[2,32,1792]{2,1,0:T(8,128)(2,1)S(1)} collective-permute-done((bf16[2,32,1792]{2,1,0:T(8,128)(2,1)S(1)}, bf16[2,32,1792]{2,1,0:T(8,128)(2,1)S(1)}, u32[]{:S(2)}, u32[]{:S(2)}) %collective-permute-start.11) | collective-permute-done | bytes 229408 | tf_op jit(solution)/shard_map/ppermute | solution.py:133
  77.5 9.8 %collective-permute-done.13 = bf16[2,32,1792]{2,1,0:T(8,128)(2,1)S(1)} collective-permute-done((bf16[2,32,1792]{2,1,0:T(8,128)(2,1)S(1)}, bf16[2,32,1792]{2,1,0:T(8,128)(2,1)S(1)}, u32[]{:S(2)}, u32[]{:S(2)}) %collective-permute-start.13) | collective-permute-done | bytes 229408 | tf_op jit(solution)/shard_map/ppermute | solution.py:133
  88.6 2.1 %collective-permute-start.16 = (bf16[2,32,1792]{2,1,0:T(8,128)(2,1)S(1)}, bf16[2,32,1792]{2,1,0:T(8,128)(2,1)}, u32[]{:S(2)}, u32[]{:S(2)}) collective-permute-start(bf16[2,32,1792]{2,1,0:T(8,128)(2,1)S(1)} %get-tuple-element.83), channel_id=1, source_target_pairs={{0,24},{8,0},{16,8},{24,16},{1,25},{9,1},{17,9},{25,17},{2,26},{10... | collective-permute-start | bytes 688136 | tf_op jit(solution)/shard_map/ppermute | solution.py:133
  96.5 2.7 %collective-permute-start.23 = (bf16[32,1792]{1,0:T(8,128)(2,1)}, bf16[32,1792]{1,0:T(8,128)(2,1)S(1)}, u32[]{:S(2)}, u32[]{:S(2)}) collective-permute-start(bf16[32,1792]{1,0:T(8,128)(2,1)} %get-tuple-element.149), channel_id=1, source_target_pairs={{0,96},{32,64},{64,32},{96,0},{1,97},{33,65},{65,33},{97,1},{2,98}... | collective-permute-start | bytes 344072 | tf_op jit(solution)/shard_map/ppermute | solution.py:156
  99.2 2.9 %collective-permute-start.24 = (bf16[32,1792]{1,0:T(8,128)(2,1)}, bf16[32,1792]{1,0:T(8,128)(2,1)S(1)}, u32[]{:S(2)}, u32[]{:S(2)}) collective-permute-start(bf16[32,1792]{1,0:T(8,128)(2,1)} %get-tuple-element.148), channel_id=1, source_target_pairs={{0,64},{32,96},{64,0},{96,32},{1,65},{33,97},{65,1},{97,33},{2,66}... | collective-permute-start | bytes 344072 | tf_op jit(solution)/shard_map/ppermute | solution.py:156
  102.3 3.2 %collective-permute-start.21 = (bf16[2,32,1792]{2,1,0:T(8,128)(2,1)S(1)}, bf16[2,32,1792]{2,1,0:T(8,128)(2,1)S(1)}, u32[]{:S(2)}, u32[]{:S(2)}) collective-permute-start(bf16[2,32,1792]{2,1,0:T(8,128)(2,1)S(1)} %get-tuple-element.101), channel_id=1, source_target_pairs={{0,24},{8,0},{16,8},{24,16},{1,25},{9,1},{17,9},{25,17},{2,26},{10... | collective-permute-start | bytes 688136 | tf_op jit(solution)/shard_map/ppermute | solution.py:133
  106.3 14.9 %shard_map.86 = (bf16[768,1792]{1,0:T(8,128)(2,1)}, bf16[768,1792]{1,0:T(8,128)(2,1)}) custom-call(s32[6]{0:T(128)} %stack.45.places, bf16[256,1536]{1,0:T(8,128)(2,1)} %copy-done.1, bf16[256,1536]{1,0:T(8,128)(2,1)} %copy-done.5, bf16[256,1536]{1,0:T(8,128)(2,1)} %copy-done.6, bf16[256,1536]{1,0:T(8,128)(2,1)} %copy-done.7, bf16[256,768]{1,0:T(8,128)(2,1)} %copy-done.11, ...), custom_call_target="tpu_custom_call" | custom-call | flops 49999998976 | tf_op jit(solution)/shard_map/pallas_call | solution.py:93
  123.3 2.8 %collective-permute-start.26 = (bf16[32,1792]{1,0:T(8,128)(2,1)S(1)}, bf16[32,1792]{1,0:T(8,128)(2,1)S(1)}, u32[]{:S(2)}, u32[]{:S(2)}) collective-permute-start(bf16[32,1792]{1,0:T(8,128)(2,1)S(1)} %get-tuple-element.146), channel_id=1, source_target_pairs={{0,96},{32,64},{64,32},{96,0},{1,97},{33,65},{65,33},{97,1},{2,98}... | collective-permute-start | bytes 344072 | tf_op jit(solution)/shard_map/ppermute | solution.py:156
  127.8 1.9 %collective-permute-done.26 = bf16[32,1792]{1,0:T(8,128)(2,1)S(1)} collective-permute-done((bf16[32,1792]{1,0:T(8,128)(2,1)S(1)}, bf16[32,1792]{1,0:T(8,128)(2,1)S(1)}, u32[]{:S(2)}, u32[]{:S(2)}) %collective-permute-start.26) | collective-permute-done | bytes 114720 | tf_op jit(solution)/shard_map/ppermute | solution.py:156
  129.7 2.7 %collective-permute-done.27 = bf16[32,1792]{1,0:T(8,128)(2,1)S(1)} collective-permute-done((bf16[32,1792]{1,0:T(8,128)(2,1)S(1)}, bf16[32,1792]{1,0:T(8,128)(2,1)S(1)}, u32[]{:S(2)}, u32[]{:S(2)}) %collective-permute-start.27) | collective-permute-done | bytes 114720 | tf_op jit(solution)/shard_map/ppermute | solution.py:156
  132.5 5.2 %collective-permute-start.28 = (bf16[32,1792]{1,0:T(8,128)(2,1)S(1)}, bf16[32,1792]{1,0:T(8,128)(2,1)S(1)}, u32[]{:S(2)}, u32[]{:S(2)}) collective-permute-start(bf16[32,1792]{1,0:T(8,128)(2,1)S(1)} %get-tuple-element.131), channel_id=1, source_target_pairs={{0,128},{128,0},{1,129},{129,1},{2,130},{130,2},{3,131},{131,3},{4... | collective-permute-start | bytes 344072 | tf_op jit(solution)/shard_map/ppermute | solution.py:207
  137.7 3.7 %collective-permute-done.28 = bf16[32,1792]{1,0:T(8,128)(2,1)S(1)} collective-permute-done((bf16[32,1792]{1,0:T(8,128)(2,1)S(1)}, bf16[32,1792]{1,0:T(8,128)(2,1)S(1)}, u32[]{:S(2)}, u32[]{:S(2)}) %collective-permute-start.28) | collective-permute-done | bytes 114720 | tf_op jit(solution)/shard_map/ppermute | solution.py:207
  (103 shorter events, 29.5 us)
Async XLA Ops:
  7.2 95.0 %all-gather.2.cloned.1.call-start = ((), (), s32[]{:S(2)}) async-start(), calls=%async_computation | async-start | bytes 7569408 | tf_op jit(solution)/shard_map/all_gather | solution.py:164
  8.7 12.5 %collective-permute-start = (bf16[256,768]{1,0:T(8,128)(2,1)S(1)}, bf16[256,768]{1,0:T(8,128)(2,1)S(1)}, u32[]{:S(2)}, u32[]{:S(2)}) collective-permute-start(bf16[256,768]{1,0:T(8,128)(2,1)S(1)} %bitcast.143), channel_id=1, source_target_pairs={{0,4},{4,0},{1,5},{5,1},{2,6},{6,2},{3,7},{7,3},{8,12},{12,8},{9,1... | collective-permute-start | bytes 1179656 | tf_op jit(solution)/shard_map/ppermute | solution.py:130
  8.8 12.6 %collective-permute-start.1 = (bf16[32,1792]{1,0:T(8,128)(2,1)S(1)}, bf16[32,1792]{1,0:T(8,128)(2,1)S(1)}, u32[]{:S(2)}, u32[]{:S(2)}) collective-permute-start(bf16[32,1792]{1,0:T(8,128)(2,1)S(1)} %copy-done.8), channel_id=1, source_target_pairs={{0,128},{128,0},{1,129},{129,1},{2,130},{130,2},{3,131},{131,3},{4... | collective-permute-start | bytes 344072 | tf_op jit(solution)/shard_map/ppermute | solution.py:160
  22.6 19.7 %collective-permute-start.2 = (bf16[256,1536]{1,0:T(8,128)(2,1)S(1)}, bf16[256,1536]{1,0:T(8,128)(2,1)S(1)}, u32[]{:S(2)}, u32[]{:S(2)}) collective-permute-start(bf16[256,1536]{1,0:T(8,128)(2,1)S(1)} %pad_maximum_fusion.refs_0_), channel_id=1, source_target_pairs={{0,1},{1,2},{2,3},{3,0},{4,5},{5,6},{6,7},{7,4},{8,9},{9,10},{10,1... | collective-permute-start | bytes 2359304 | tf_op jit(solution)/shard_map/ppermute | solution.py:127
  42.3 19.7 %collective-permute-start.5 = (bf16[256,1536]{1,0:T(8,128)(2,1)S(1)}, bf16[256,1536]{1,0:T(8,128)(2,1)S(1)}, u32[]{:S(2)}, u32[]{:S(2)}) collective-permute-start(bf16[256,1536]{1,0:T(8,128)(2,1)S(1)} %collective-permute-done.2.refs_1_), channel_id=1, source_target_pairs={{0,1},{1,2},{2,3},{3,0},{4,5},{5,6},{6,7},{7,4},{8,9},{9,10},{10,1... | collective-permute-start | bytes 2359304 | tf_op jit(solution)/shard_map/ppermute | solution.py:127
  43.6 9.1 %collective-permute-start.6 = (bf16[2,32,1792]{2,1,0:T(8,128)(2,1)S(1)}, bf16[2,32,1792]{2,1,0:T(8,128)(2,1)S(1)}, u32[]{:S(2)}, u32[]{:S(2)}) collective-permute-start(bf16[2,32,1792]{2,1,0:T(8,128)(2,1)S(1)} %get-tuple-element.73), channel_id=1, source_target_pairs={{0,8},{8,16},{16,24},{24,0},{1,9},{9,17},{17,25},{25,1},{2,10},{10... | collective-permute-start | bytes 688136 | tf_op jit(solution)/shard_map/ppermute | solution.py:133
  45.3 8.4 %collective-permute-start.7 = (bf16[2,32,1792]{2,1,0:T(8,128)(2,1)S(1)}, bf16[2,32,1792]{2,1,0:T(8,128)(2,1)S(1)}, u32[]{:S(2)}, u32[]{:S(2)}) collective-permute-start(bf16[2,32,1792]{2,1,0:T(8,128)(2,1)S(1)} %get-tuple-element.74), channel_id=1, source_target_pairs={{0,24},{8,0},{16,8},{24,16},{1,25},{9,1},{17,9},{25,17},{2,26},{10... | collective-permute-start | bytes 688136 | tf_op jit(solution)/shard_map/ppermute | solution.py:133
  46.9 11.8 %collective-permute-start.8 = (bf16[2,32,1792]{2,1,0:T(8,128)(2,1)S(1)}, bf16[2,32,1792]{2,1,0:T(8,128)(2,1)S(1)}, u32[]{:S(2)}, u32[]{:S(2)}) collective-permute-start(bf16[2,32,1792]{2,1,0:T(8,128)(2,1)S(1)} %get-tuple-element.75), channel_id=1, source_target_pairs={{0,16},{8,24},{16,0},{24,8},{1,17},{9,25},{17,1},{25,9},{2,18},{10... | collective-permute-start | bytes 688136 | tf_op jit(solution)/shard_map/ppermute | solution.py:133
  49.0 9.7 %collective-permute-start.9 = (bf16[256,768]{1,0:T(8,128)(2,1)S(1)}, bf16[256,768]{1,0:T(8,128)(2,1)S(1)}, u32[]{:S(2)}, u32[]{:S(2)}) collective-permute-start(bf16[256,768]{1,0:T(8,128)(2,1)S(1)} %slice.42), channel_id=1, source_target_pairs={{0,4},{4,0},{1,5},{5,1},{2,6},{6,2},{3,7},{7,3},{8,12},{12,8},{9,1... | collective-permute-start | bytes 1179656 | tf_op jit(solution)/shard_map/ppermute | solution.py:130
  62.0 25.3 %collective-permute-start.10 = (bf16[256,1536]{1,0:T(8,128)(2,1)S(1)}, bf16[256,1536]{1,0:T(8,128)(2,1)S(1)}, u32[]{:S(2)}, u32[]{:S(2)}) collective-permute-start(bf16[256,1536]{1,0:T(8,128)(2,1)S(1)} %collective-permute-done.5.refs_2_), channel_id=1, source_target_pairs={{0,1},{1,2},{2,3},{3,0},{4,5},{5,6},{6,7},{7,4},{8,9},{9,10},{10,1... | collective-permute-start | bytes 2359304 | tf_op jit(solution)/shard_map/ppermute | solution.py:127
  62.4 14.2 %collective-permute-start.11 = (bf16[2,32,1792]{2,1,0:T(8,128)(2,1)S(1)}, bf16[2,32,1792]{2,1,0:T(8,128)(2,1)S(1)}, u32[]{:S(2)}, u32[]{:S(2)}) collective-permute-start(bf16[2,32,1792]{2,1,0:T(8,128)(2,1)S(1)} %get-tuple-element.78), channel_id=1, source_target_pairs={{0,8},{8,16},{16,24},{24,0},{1,9},{9,17},{17,25},{25,1},{2,10},{10... | collective-permute-start | bytes 688136 | tf_op jit(solution)/shard_map/ppermute | solution.py:133
  64.2 13.3 %collective-permute-start.12 = (bf16[2,32,1792]{2,1,0:T(8,128)(2,1)S(1)}, bf16[2,32,1792]{2,1,0:T(8,128)(2,1)S(1)}, u32[]{:S(2)}, u32[]{:S(2)}) collective-permute-start(bf16[2,32,1792]{2,1,0:T(8,128)(2,1)S(1)} %get-tuple-element.79), channel_id=1, source_target_pairs={{0,24},{8,0},{16,8},{24,16},{1,25},{9,1},{17,9},{25,17},{2,26},{10... | collective-permute-start | bytes 688136 | tf_op jit(solution)/shard_map/ppermute | solution.py:133
  65.8 21.6 %collective-permute-start.13 = (bf16[2,32,1792]{2,1,0:T(8,128)(2,1)S(1)}, bf16[2,32,1792]{2,1,0:T(8,128)(2,1)S(1)}, u32[]{:S(2)}, u32[]{:S(2)}) collective-permute-start(bf16[2,32,1792]{2,1,0:T(8,128)(2,1)S(1)} %get-tuple-element.80), channel_id=1, source_target_pairs={{0,16},{8,24},{16,0},{24,8},{1,17},{9,25},{17,1},{25,9},{2,18},{10... | collective-permute-start | bytes 688136 | tf_op jit(solution)/shard_map/ppermute | solution.py:133
  67.8 19.5 %collective-permute-start.14 = (bf16[256,768]{1,0:T(8,128)(2,1)S(1)}, bf16[256,768]{1,0:T(8,128)(2,1)S(1)}, u32[]{:S(2)}, u32[]{:S(2)}) collective-permute-start(bf16[256,768]{1,0:T(8,128)(2,1)S(1)} %slice.44), channel_id=1, source_target_pairs={{0,4},{4,0},{1,5},{5,1},{2,6},{6,2},{3,7},{7,3},{8,12},{12,8},{9,1... | collective-permute-start | bytes 1179656 | tf_op jit(solution)/shard_map/ppermute | solution.py:130
  87.4 11.8 %collective-permute-start.15 = (bf16[2,32,1792]{2,1,0:T(8,128)(2,1)S(1)}, bf16[2,32,1792]{2,1,0:T(8,128)(2,1)S(1)}, u32[]{:S(2)}, u32[]{:S(2)}) collective-permute-start(bf16[2,32,1792]{2,1,0:T(8,128)(2,1)S(1)} %get-tuple-element.82), channel_id=1, source_target_pairs={{0,8},{8,16},{16,24},{24,0},{1,9},{9,17},{17,25},{25,1},{2,10},{10... | collective-permute-start | bytes 688136 | tf_op jit(solution)/shard_map/ppermute | solution.py:133
  88.6 13.6 %collective-permute-start.16 = (bf16[2,32,1792]{2,1,0:T(8,128)(2,1)S(1)}, bf16[2,32,1792]{2,1,0:T(8,128)(2,1)}, u32[]{:S(2)}, u32[]{:S(2)}) collective-permute-start(bf16[2,32,1792]{2,1,0:T(8,128)(2,1)S(1)} %get-tuple-element.83), channel_id=1, source_target_pairs={{0,24},{8,0},{16,8},{24,16},{1,25},{9,1},{17,9},{25,17},{2,26},{10... | collective-permute-start | bytes 688136 | tf_op jit(solution)/shard_map/ppermute | solution.py:133
  90.7 11.5 %collective-permute-start.17 = (bf16[2,32,1792]{2,1,0:T(8,128)(2,1)S(1)}, bf16[2,32,1792]{2,1,0:T(8,128)(2,1)}, u32[]{:S(2)}, u32[]{:S(2)}) collective-permute-start(bf16[2,32,1792]{2,1,0:T(8,128)(2,1)S(1)} %get-tuple-element.84), channel_id=1, source_target_pairs={{0,16},{8,24},{16,0},{24,8},{1,17},{9,25},{17,1},{25,9},{2,18},{10... | collective-permute-start | bytes 688136 | tf_op jit(solution)/shard_map/ppermute | solution.py:133
  93.2 9.0 %collective-permute-start.19 = (bf16[256,768]{1,0:T(8,128)(2,1)S(1)}, bf16[256,768]{1,0:T(8,128)(2,1)}, u32[]{:S(2)}, u32[]{:S(2)}) collective-permute-start(bf16[256,768]{1,0:T(8,128)(2,1)S(1)} %slice.47), channel_id=1, source_target_pairs={{0,4},{4,0},{1,5},{5,1},{2,6},{6,2},{3,7},{7,3},{8,12},{12,8},{9,1... | collective-permute-start | bytes 1179656 | tf_op jit(solution)/shard_map/ppermute | solution.py:130
  96.5 25.9 %collective-permute-start.23 = (bf16[32,1792]{1,0:T(8,128)(2,1)}, bf16[32,1792]{1,0:T(8,128)(2,1)S(1)}, u32[]{:S(2)}, u32[]{:S(2)}) collective-permute-start(bf16[32,1792]{1,0:T(8,128)(2,1)} %get-tuple-element.149), channel_id=1, source_target_pairs={{0,96},{32,64},{64,32},{96,0},{1,97},{33,65},{65,33},{97,1},{2,98}... | collective-permute-start | bytes 344072 | tf_op jit(solution)/shard_map/ppermute | solution.py:156
  99.2 23.2 %collective-permute-start.24 = (bf16[32,1792]{1,0:T(8,128)(2,1)}, bf16[32,1792]{1,0:T(8,128)(2,1)S(1)}, u32[]{:S(2)}, u32[]{:S(2)}) collective-permute-start(bf16[32,1792]{1,0:T(8,128)(2,1)} %get-tuple-element.148), channel_id=1, source_target_pairs={{0,64},{32,96},{64,0},{96,32},{1,65},{33,97},{65,1},{97,33},{2,66}... | collective-permute-start | bytes 344072 | tf_op jit(solution)/shard_map/ppermute | solution.py:156
  102.2 20.2 %collective-permute-start.20 = (bf16[2,32,1792]{2,1,0:T(8,128)(2,1)S(1)}, bf16[2,32,1792]{2,1,0:T(8,128)(2,1)S(1)}, u32[]{:S(2)}, u32[]{:S(2)}) collective-permute-start(bf16[2,32,1792]{2,1,0:T(8,128)(2,1)S(1)} %get-tuple-element.100), channel_id=1, source_target_pairs={{0,8},{8,16},{16,24},{24,0},{1,9},{9,17},{17,25},{25,1},{2,10},{10... | collective-permute-start | bytes 688136 | tf_op jit(solution)/shard_map/ppermute | solution.py:133
  102.3 20.1 %collective-permute-start.21 = (bf16[2,32,1792]{2,1,0:T(8,128)(2,1)S(1)}, bf16[2,32,1792]{2,1,0:T(8,128)(2,1)S(1)}, u32[]{:S(2)}, u32[]{:S(2)}) collective-permute-start(bf16[2,32,1792]{2,1,0:T(8,128)(2,1)S(1)} %get-tuple-element.101), channel_id=1, source_target_pairs={{0,24},{8,0},{16,8},{24,16},{1,25},{9,1},{17,9},{25,17},{2,26},{10... | collective-permute-start | bytes 688136 | tf_op jit(solution)/shard_map/ppermute | solution.py:133
  105.5 16.9 %collective-permute-start.22 = (bf16[2,32,1792]{2,1,0:T(8,128)(2,1)S(1)}, bf16[2,32,1792]{2,1,0:T(8,128)(2,1)S(1)}, u32[]{:S(2)}, u32[]{:S(2)}) collective-permute-start(bf16[2,32,1792]{2,1,0:T(8,128)(2,1)S(1)} %get-tuple-element.102), channel_id=1, source_target_pairs={{0,16},{8,24},{16,0},{24,8},{1,17},{9,25},{17,1},{25,9},{2,18},{10... | collective-permute-start | bytes 688136 | tf_op jit(solution)/shard_map/ppermute | solution.py:133
  132.5 8.9 %collective-permute-start.28 = (bf16[32,1792]{1,0:T(8,128)(2,1)S(1)}, bf16[32,1792]{1,0:T(8,128)(2,1)S(1)}, u32[]{:S(2)}, u32[]{:S(2)}) collective-permute-start(bf16[32,1792]{1,0:T(8,128)(2,1)S(1)} %get-tuple-element.131), channel_id=1, source_target_pairs={{0,128},{128,0},{1,129},{129,1},{2,130},{130,2},{3,131},{131,3},{4... | collective-permute-start | bytes 344072 | tf_op jit(solution)/shard_map/ppermute | solution.py:207
  (20 other events, 137.5 us)
Sparse Core Ops, SparseCore 0:
  22.4 67.0 all-gather.1

commit v3 on v2

--- a/solution.py
+++ b/solution.py
@@ -30,22 +30,25 @@
     return pl.CostEstimate(flops=int(seconds * 1e15), bytes_accessed=0, transcendentals=0)
 
 
-def column(row):
+def column(scale, at):
+    row = scale[pl.ds(at, BLOCK)].reshape(1, BLOCK)
     return jnp.broadcast_to(row, (8, BLOCK)).T[:, :1]
 
 
 def hidden_kernel(gate_codes, up_codes, gate_scale, up_scale, out):
-    for i in range(gate_scale.shape[0]):
-        rows = slice(i * BLOCK, (i + 1) * BLOCK)
-        g = gate_codes[rows, :].astype(F32) * column(gate_scale[i])
-        u = up_codes[rows, :].astype(F32) * column(up_scale[i])
+    tokens = out.shape[0]
+    for i in range(0, tokens, BLOCK):
+        rows = slice(i, i + BLOCK)
+        at = pl.multiple_of(pl.program_id(0) * tokens + i, BLOCK)
+        g = gate_codes[rows, :].astype(F32) * column(gate_scale, at)
+        u = up_codes[rows, :].astype(F32) * column(up_scale, at)
         out[rows, :] = (g * jax.nn.sigmoid(g) * u).astype(BF)
 
 
 def hidden_of(gate_codes, up_codes, gate_scale, up_scale):
     tokens, cols = gate_codes.shape
     rows = pl.BlockSpec((tokens // 2, cols), lambda i: (i, 0))
-    scale = pl.BlockSpec((tokens // 2 // BLOCK, 1, BLOCK), lambda i: (i, 0, 0))
+    scale = pl.BlockSpec((tokens,), lambda i: (0,))
     return pl.pallas_call(
         hidden_kernel,
         grid=(2,),
@@ -70,7 +73,7 @@
             rows[k, 1] = others[k][...].T
         for i in range(tokens // BLOCK):
             for j, scale in enumerate((gate_scale, up_scale)):
-                scales[j, i * BLOCK : (i + 1) * BLOCK, :] = column(scale[i])
+                scales[j, i * BLOCK : (i + 1) * BLOCK, :] = column(scale, i * BLOCK)
 
     grad = None
     for k in range(4):
@@ -116,7 +119,7 @@
     zh, x, y, c, t = (lax.axis_index(n) for n in ("zh", "x", "y", "c", "t"))
     tokens, cols = gate_codes.shape
     normalizer = 1.0 / math.sqrt(tokens * 64)
-    codes = (gate_codes, up_codes, gate_scale.reshape(-1, 1, BLOCK), up_scale.reshape(-1, 1, BLOCK))
+    codes = (gate_codes, up_codes, gate_scale, up_scale)
 
     bar = lax.optimization_barrier
 

time: 150 us -> 149 us (level)
    ppermute x6, starting transfers between devices: 11.3 us -> 9.08 us  [over_x(): return [lax.ppermute(rows(m).astype(BF), 'x', flip(4, m)) for m in places]]
    ppermute x12, starting transfers between devices: 17.5 us -> 19.7 us  [over_y(): lax.ppermute(b, 'y', shift(4, d))]
where the time goes in v3:
time: 149 us
  waiting for transfers between devices  55 us (37%)
  starting transfers between devices  44.8 us (30%)
  Pallas kernels  19.7 us (13%)
  between operations  14.8 us (10%)
  matrix products  7.08 us (5%)
  other arithmetic  4.09 us (3%)
  local copies, waits for them, and re-layouts  3.43 us (2%)
    ppermute x12, waiting for transfers between devices, over_y(): lax.ppermute(b, 'y', shift(4, d))  24.5 us
    ppermute x12, starting transfers between devices, over_y(): lax.ppermute(b, 'y', shift(4, d))  19.7 us
    ppermute x3, waiting for transfers between devices, ring(): return lax.ppermute(slot, 't', shift(4, 1))  15.1 us
    pallas_call x1, Pallas kernels, grads_of(): pl.pallas_call(grads_kernel, grid_spec=pltpu.PrefetchScalarGridSpec(num_s...  14.9 us
    ppermute x6, starting transfers between devices, over_x(): return [lax.ppermute(rows(m).astype(BF), 'x', flip(4, m)) for m in places]  9.08 us
    ppermute x6, waiting for transfers between devices, over_x(): return [lax.ppermute(rows(m).astype(BF), 'x', flip(4, m)) for m in places]  6.88 us
    ppermute x1, starting transfers between devices, on_device(): peer = lax.ppermute(after(weight, sent), 'zh', shift(2, 1))  6.38 us
    ppermute x1, starting transfers between devices, on_device(): lax.ppermute(jnp.where(here, second, first).astype(BF), 'zh', shift(2, 1))  5.19 us
  transfers between devices with their start and end apart: 30, of which 15 were waited for; matrix products, arithmetic and copies ran while one was open for 8% of the time, Pallas kernels for 13%

profile of v3, /device:TPU:32, one launch (start us, length us, event | category | flops | bytes accessed | tf_op | source)
XLA Modules:
  0.0 148.9 jit_solution(462500642975493670)
XLA Ops:
  8.8 6.4 %collective-permute-start.1 = (bf16[32,1792]{1,0:T(8,128)(2,1)S(1)}, bf16[32,1792]{1,0:T(8,128)(2,1)S(1)}, u32[]{:S(2)}, u32[]{:S(2)}) collective-permute-start(bf16[32,1792]{1,0:T(8,128)(2,1)S(1)} %copy-done.8), channel_id=1, source_target_pairs={{0,128},{128,0},{1,129},{129,1},{2,130},{130,2},{3,131},{131,3},{4... | collective-permute-start | bytes 344072 | tf_op jit(solution)/shard_map/ppermute | solution.py:163
  15.2 4.8 %shard_map.85 = bf16[768,1792]{1,0:T(8,128)(2,1)} custom-call(bf16[768,1792]{1,0:T(8,128)(2,1)} %refs_9_.1, bf16[768,1792]{1,0:T(8,128)(2,1)} %refs_10_.1, f32[768]{0:T(1024)} %refs_11_.1, f32[768]{0:T(1024)} %refs_12_.1), custom_call_target="tpu_custom_call" | custom-call | flops 49999998976 | tf_op jit(solution)/shard_map/pallas_call | solution.py:52
  24.0 3.5 %collective-permute-done.3 = bf16[768,1792]{1,0:T(8,128)(2,1)S(1)} collective-permute-done((bf16[768,1792]{1,0:T(8,128)(2,1)}, bf16[768,1792]{1,0:T(8,128)(2,1)S(1)}, u32[]{:S(2)}, u32[]{:S(2)}) %collective-permute-start.3) | collective-permute-done | bytes 2752544 | tf_op jit(solution)/shard_map/ppermute | solution.py:133
  29.5 12.7 %collective-permute-done.2.refs_1_ = bf16[256,1536]{1,0:T(8,128)(2,1)S(1)} collective-permute-done((bf16[256,1536]{1,0:T(8,128)(2,1)S(1)}, bf16[256,1536]{1,0:T(8,128)(2,1)S(1)}, u32[]{:S(2)}, u32[]{:S(2)}) %collective-permute-start.2) | collective-permute-done | bytes 786464 | tf_op jit(solution)/shard_map/ppermute | solution.py:130
  43.5 1.7 %collective-permute-start.6 = (bf16[2,32,1792]{2,1,0:T(8,128)(2,1)S(1)}, bf16[2,32,1792]{2,1,0:T(8,128)(2,1)S(1)}, u32[]{:S(2)}, u32[]{:S(2)}) collective-permute-start(bf16[2,32,1792]{2,1,0:T(8,128)(2,1)S(1)} %get-tuple-element.73), channel_id=1, source_target_pairs={{0,8},{8,16},{16,24},{24,0},{1,9},{9,17},{17,25},{25,1},{2,10},{10... | collective-permute-start | bytes 688136 | tf_op jit(solution)/shard_map/ppermute | solution.py:136
  45.3 1.6 %collective-permute-start.7 = (bf16[2,32,1792]{2,1,0:T(8,128)(2,1)S(1)}, bf16[2,32,1792]{2,1,0:T(8,128)(2,1)S(1)}, u32[]{:S(2)}, u32[]{:S(2)}) collective-permute-start(bf16[2,32,1792]{2,1,0:T(8,128)(2,1)S(1)} %get-tuple-element.74), channel_id=1, source_target_pairs={{0,24},{8,0},{16,8},{24,16},{1,25},{9,1},{17,9},{25,17},{2,26},{10... | collective-permute-start | bytes 688136 | tf_op jit(solution)/shard_map/ppermute | solution.py:136
  46.9 2.1 %collective-permute-start.8 = (bf16[2,32,1792]{2,1,0:T(8,128)(2,1)S(1)}, bf16[2,32,1792]{2,1,0:T(8,128)(2,1)S(1)}, u32[]{:S(2)}, u32[]{:S(2)}) collective-permute-start(bf16[2,32,1792]{2,1,0:T(8,128)(2,1)S(1)} %get-tuple-element.75), channel_id=1, source_target_pairs={{0,16},{8,24},{16,0},{24,8},{1,17},{9,25},{17,1},{25,9},{2,18},{10... | collective-permute-start | bytes 688136 | tf_op jit(solution)/shard_map/ppermute | solution.py:136
  50.9 1.8 %collective-permute-done.6 = bf16[2,32,1792]{2,1,0:T(8,128)(2,1)S(1)} collective-permute-done((bf16[2,32,1792]{2,1,0:T(8,128)(2,1)S(1)}, bf16[2,32,1792]{2,1,0:T(8,128)(2,1)S(1)}, u32[]{:S(2)}, u32[]{:S(2)}) %collective-permute-start.6) | collective-permute-done | bytes 229408 | tf_op jit(solution)/shard_map/ppermute | solution.py:136
  53.7 4.9 %collective-permute-done.8 = bf16[2,32,1792]{2,1,0:T(8,128)(2,1)S(1)} collective-permute-done((bf16[2,32,1792]{2,1,0:T(8,128)(2,1)S(1)}, bf16[2,32,1792]{2,1,0:T(8,128)(2,1)S(1)}, u32[]{:S(2)}, u32[]{:S(2)}) %collective-permute-start.8) | collective-permute-done | bytes 229408 | tf_op jit(solution)/shard_map/ppermute | solution.py:136
  58.7 2.4 %collective-permute-done.5.refs_2_ = bf16[256,1536]{1,0:T(8,128)(2,1)S(1)} collective-permute-done((bf16[256,1536]{1,0:T(8,128)(2,1)S(1)}, bf16[256,1536]{1,0:T(8,128)(2,1)S(1)}, u32[]{:S(2)}, u32[]{:S(2)}) %collective-permute-start.5) | collective-permute-done | bytes 786464 | tf_op jit(solution)/shard_map/ppermute | solution.py:130
  62.4 1.7 %collective-permute-start.11 = (bf16[2,32,1792]{2,1,0:T(8,128)(2,1)S(1)}, bf16[2,32,1792]{2,1,0:T(8,128)(2,1)S(1)}, u32[]{:S(2)}, u32[]{:S(2)}) collective-permute-start(bf16[2,32,1792]{2,1,0:T(8,128)(2,1)S(1)} %get-tuple-element.78), channel_id=1, source_target_pairs={{0,8},{8,16},{16,24},{24,0},{1,9},{9,17},{17,25},{25,1},{2,10},{10... | collective-permute-start | bytes 688136 | tf_op jit(solution)/shard_map/ppermute | solution.py:136
  65.7 2.1 %collective-permute-start.13 = (bf16[2,32,1792]{2,1,0:T(8,128)(2,1)S(1)}, bf16[2,32,1792]{2,1,0:T(8,128)(2,1)S(1)}, u32[]{:S(2)}, u32[]{:S(2)}) collective-permute-start(bf16[2,32,1792]{2,1,0:T(8,128)(2,1)S(1)} %get-tuple-element.80), channel_id=1, source_target_pairs={{0,16},{8,24},{16,0},{24,8},{1,17},{9,25},{17,1},{25,9},{2,18},{10... | collective-permute-start | bytes 688136 | tf_op jit(solution)/shard_map/ppermute | solution.py:136
  70.6 6.0 %collective-permute-done.11 = bf16[2,32,1792]{2,1,0:T(8,128)(2,1)S(1)} collective-permute-done((bf16[2,32,1792]{2,1,0:T(8,128)(2,1)S(1)}, bf16[2,32,1792]{2,1,0:T(8,128)(2,1)S(1)}, u32[]{:S(2)}, u32[]{:S(2)}) %collective-permute-start.11) | collective-permute-done | bytes 229408 | tf_op jit(solution)/shard_map/ppermute | solution.py:136
  77.5 9.8 %collective-permute-done.13 = bf16[2,32,1792]{2,1,0:T(8,128)(2,1)S(1)} collective-permute-done((bf16[2,32,1792]{2,1,0:T(8,128)(2,1)S(1)}, bf16[2,32,1792]{2,1,0:T(8,128)(2,1)S(1)}, u32[]{:S(2)}, u32[]{:S(2)}) %collective-permute-start.13) | collective-permute-done | bytes 229408 | tf_op jit(solution)/shard_map/ppermute | solution.py:136
  88.5 2.1 %collective-permute-start.16 = (bf16[2,32,1792]{2,1,0:T(8,128)(2,1)S(1)}, bf16[2,32,1792]{2,1,0:T(8,128)(2,1)}, u32[]{:S(2)}, u32[]{:S(2)}) collective-permute-start(bf16[2,32,1792]{2,1,0:T(8,128)(2,1)S(1)} %get-tuple-element.83), channel_id=1, source_target_pairs={{0,24},{8,0},{16,8},{24,16},{1,25},{9,1},{17,9},{25,17},{2,26},{10... | collective-permute-start | bytes 688136 | tf_op jit(solution)/shard_map/ppermute | solution.py:136
  96.4 2.7 %collective-permute-start.23 = (bf16[32,1792]{1,0:T(8,128)(2,1)}, bf16[32,1792]{1,0:T(8,128)(2,1)S(1)}, u32[]{:S(2)}, u32[]{:S(2)}) collective-permute-start(bf16[32,1792]{1,0:T(8,128)(2,1)} %get-tuple-element.149), channel_id=1, source_target_pairs={{0,96},{32,64},{64,32},{96,0},{1,97},{33,65},{65,33},{97,1},{2,98}... | collective-permute-start | bytes 344072 | tf_op jit(solution)/shard_map/ppermute | solution.py:159
  101.3 2.0 %collective-permute-start.21 = (bf16[2,32,1792]{2,1,0:T(8,128)(2,1)S(1)}, bf16[2,32,1792]{2,1,0:T(8,128)(2,1)S(1)}, u32[]{:S(2)}, u32[]{:S(2)}) collective-permute-start(bf16[2,32,1792]{2,1,0:T(8,128)(2,1)S(1)} %get-tuple-element.101), channel_id=1, source_target_pairs={{0,24},{8,0},{16,8},{24,16},{1,25},{9,1},{17,9},{25,17},{2,26},{10... | collective-permute-start | bytes 688136 | tf_op jit(solution)/shard_map/ppermute | solution.py:136
  103.3 2.2 %collective-permute-start.22 = (bf16[2,32,1792]{2,1,0:T(8,128)(2,1)S(1)}, bf16[2,32,1792]{2,1,0:T(8,128)(2,1)S(1)}, u32[]{:S(2)}, u32[]{:S(2)}) collective-permute-start(bf16[2,32,1792]{2,1,0:T(8,128)(2,1)S(1)} %get-tuple-element.102), channel_id=1, source_target_pairs={{0,16},{8,24},{16,0},{24,8},{1,17},{9,25},{17,1},{25,9},{2,18},{10... | collective-permute-start | bytes 688136 | tf_op jit(solution)/shard_map/ppermute | solution.py:136
  106.2 14.9 %shard_map.86 = (bf16[768,1792]{1,0:T(8,128)(2,1)}, bf16[768,1792]{1,0:T(8,128)(2,1)}) custom-call(s32[6]{0:T(128)} %stack.45.places, bf16[256,1536]{1,0:T(8,128)(2,1)} %copy-done.1, bf16[256,1536]{1,0:T(8,128)(2,1)} %copy-done.5, bf16[256,1536]{1,0:T(8,128)(2,1)} %copy-done.6, bf16[256,1536]{1,0:T(8,128)(2,1)} %copy-done.7, bf16[256,768]{1,0:T(8,128)(2,1)} %copy-done.9, ...), custom_call_target="tpu_custom_call" | custom-call | flops 49999998976 | tf_op jit(solution)/shard_map/pallas_call | solution.py:96
  123.3 2.8 %collective-permute-start.26 = (bf16[32,1792]{1,0:T(8,128)(2,1)S(1)}, bf16[32,1792]{1,0:T(8,128)(2,1)S(1)}, u32[]{:S(2)}, u32[]{:S(2)}) collective-permute-start(bf16[32,1792]{1,0:T(8,128)(2,1)S(1)} %get-tuple-element.146), channel_id=1, source_target_pairs={{0,96},{32,64},{64,32},{96,0},{1,97},{33,65},{65,33},{97,1},{2,98}... | collective-permute-start | bytes 344072 | tf_op jit(solution)/shard_map/ppermute | solution.py:159
  127.7 1.9 %collective-permute-done.26 = bf16[32,1792]{1,0:T(8,128)(2,1)S(1)} collective-permute-done((bf16[32,1792]{1,0:T(8,128)(2,1)S(1)}, bf16[32,1792]{1,0:T(8,128)(2,1)S(1)}, u32[]{:S(2)}, u32[]{:S(2)}) %collective-permute-start.26) | collective-permute-done | bytes 114720 | tf_op jit(solution)/shard_map/ppermute | solution.py:159
  129.6 2.7 %collective-permute-done.27 = bf16[32,1792]{1,0:T(8,128)(2,1)S(1)} collective-permute-done((bf16[32,1792]{1,0:T(8,128)(2,1)S(1)}, bf16[32,1792]{1,0:T(8,128)(2,1)S(1)}, u32[]{:S(2)}, u32[]{:S(2)}) %collective-permute-start.27) | collective-permute-done | bytes 114720 | tf_op jit(solution)/shard_map/ppermute | solution.py:159
  132.5 5.2 %collective-permute-start.28 = (bf16[32,1792]{1,0:T(8,128)(2,1)S(1)}, bf16[32,1792]{1,0:T(8,128)(2,1)S(1)}, u32[]{:S(2)}, u32[]{:S(2)}) collective-permute-start(bf16[32,1792]{1,0:T(8,128)(2,1)S(1)} %get-tuple-element.131), channel_id=1, source_target_pairs={{0,128},{128,0},{1,129},{129,1},{2,130},{130,2},{3,131},{131,3},{4... | collective-permute-start | bytes 344072 | tf_op jit(solution)/shard_map/ppermute | solution.py:210
  137.6 3.7 %collective-permute-done.28 = bf16[32,1792]{1,0:T(8,128)(2,1)S(1)} collective-permute-done((bf16[32,1792]{1,0:T(8,128)(2,1)S(1)}, bf16[32,1792]{1,0:T(8,128)(2,1)S(1)}, u32[]{:S(2)}, u32[]{:S(2)}) %collective-permute-start.28) | collective-permute-done | bytes 114720 | tf_op jit(solution)/shard_map/ppermute | solution.py:210
  (97 shorter events, 32.3 us)
Async XLA Ops:
  7.2 92.8 %all-gather.2.cloned.1.call-start = ((), (), s32[]{:S(2)}) async-start(), calls=%async_computation | async-start | bytes 7569408 | tf_op jit(solution)/shard_map/all_gather | solution.py:167
  8.7 11.3 %collective-permute-start = (bf16[256,768]{1,0:T(8,128)(2,1)S(1)}, bf16[256,768]{1,0:T(8,128)(2,1)S(1)}, u32[]{:S(2)}, u32[]{:S(2)}) collective-permute-start(bf16[256,768]{1,0:T(8,128)(2,1)S(1)} %bitcast.143), channel_id=1, source_target_pairs={{0,4},{4,0},{1,5},{5,1},{2,6},{6,2},{3,7},{7,3},{8,12},{12,8},{9,1... | collective-permute-start | bytes 1179656 | tf_op jit(solution)/shard_map/ppermute | solution.py:133
  8.8 12.6 %collective-permute-start.1 = (bf16[32,1792]{1,0:T(8,128)(2,1)S(1)}, bf16[32,1792]{1,0:T(8,128)(2,1)S(1)}, u32[]{:S(2)}, u32[]{:S(2)}) collective-permute-start(bf16[32,1792]{1,0:T(8,128)(2,1)S(1)} %copy-done.8), channel_id=1, source_target_pairs={{0,128},{128,0},{1,129},{129,1},{2,130},{130,2},{3,131},{131,3},{4... | collective-permute-start | bytes 344072 | tf_op jit(solution)/shard_map/ppermute | solution.py:163
  22.5 19.7 %collective-permute-start.2 = (bf16[256,1536]{1,0:T(8,128)(2,1)S(1)}, bf16[256,1536]{1,0:T(8,128)(2,1)S(1)}, u32[]{:S(2)}, u32[]{:S(2)}) collective-permute-start(bf16[256,1536]{1,0:T(8,128)(2,1)S(1)} %pad_maximum_fusion.refs_0_), channel_id=1, source_target_pairs={{0,1},{1,2},{2,3},{3,0},{4,5},{5,6},{6,7},{7,4},{8,9},{9,10},{10,1... | collective-permute-start | bytes 2359304 | tf_op jit(solution)/shard_map/ppermute | solution.py:130
  42.2 18.9 %collective-permute-start.5 = (bf16[256,1536]{1,0:T(8,128)(2,1)S(1)}, bf16[256,1536]{1,0:T(8,128)(2,1)S(1)}, u32[]{:S(2)}, u32[]{:S(2)}) collective-permute-start(bf16[256,1536]{1,0:T(8,128)(2,1)S(1)} %collective-permute-done.2.refs_1_), channel_id=1, source_target_pairs={{0,1},{1,2},{2,3},{3,0},{4,5},{5,6},{6,7},{7,4},{8,9},{9,10},{10,1... | collective-permute-start | bytes 2359304 | tf_op jit(solution)/shard_map/ppermute | solution.py:130
  43.5 9.1 %collective-permute-start.6 = (bf16[2,32,1792]{2,1,0:T(8,128)(2,1)S(1)}, bf16[2,32,1792]{2,1,0:T(8,128)(2,1)S(1)}, u32[]{:S(2)}, u32[]{:S(2)}) collective-permute-start(bf16[2,32,1792]{2,1,0:T(8,128)(2,1)S(1)} %get-tuple-element.73), channel_id=1, source_target_pairs={{0,8},{8,16},{16,24},{24,0},{1,9},{9,17},{17,25},{25,1},{2,10},{10... | collective-permute-start | bytes 688136 | tf_op jit(solution)/shard_map/ppermute | solution.py:136
  45.3 8.4 %collective-permute-start.7 = (bf16[2,32,1792]{2,1,0:T(8,128)(2,1)S(1)}, bf16[2,32,1792]{2,1,0:T(8,128)(2,1)S(1)}, u32[]{:S(2)}, u32[]{:S(2)}) collective-permute-start(bf16[2,32,1792]{2,1,0:T(8,128)(2,1)S(1)} %get-tuple-element.74), channel_id=1, source_target_pairs={{0,24},{8,0},{16,8},{24,16},{1,25},{9,1},{17,9},{25,17},{2,26},{10... | collective-permute-start | bytes 688136 | tf_op jit(solution)/shard_map/ppermute | solution.py:136
  46.9 11.8 %collective-permute-start.8 = (bf16[2,32,1792]{2,1,0:T(8,128)(2,1)S(1)}, bf16[2,32,1792]{2,1,0:T(8,128)(2,1)S(1)}, u32[]{:S(2)}, u32[]{:S(2)}) collective-permute-start(bf16[2,32,1792]{2,1,0:T(8,128)(2,1)S(1)} %get-tuple-element.75), channel_id=1, source_target_pairs={{0,16},{8,24},{16,0},{24,8},{1,17},{9,25},{17,1},{25,9},{2,18},{10... | collective-permute-start | bytes 688136 | tf_op jit(solution)/shard_map/ppermute | solution.py:136
  48.9 9.7 %collective-permute-start.9 = (bf16[256,768]{1,0:T(8,128)(2,1)S(1)}, bf16[256,768]{1,0:T(8,128)(2,1)S(1)}, u32[]{:S(2)}, u32[]{:S(2)}) collective-permute-start(bf16[256,768]{1,0:T(8,128)(2,1)S(1)} %slice.42), channel_id=1, source_target_pairs={{0,4},{4,0},{1,5},{5,1},{2,6},{6,2},{3,7},{7,3},{8,12},{12,8},{9,1... | collective-permute-start | bytes 1179656 | tf_op jit(solution)/shard_map/ppermute | solution.py:133
  61.1 26.2 %collective-permute-start.10 = (bf16[256,1536]{1,0:T(8,128)(2,1)S(1)}, bf16[256,1536]{1,0:T(8,128)(2,1)S(1)}, u32[]{:S(2)}, u32[]{:S(2)}) collective-permute-start(bf16[256,1536]{1,0:T(8,128)(2,1)S(1)} %collective-permute-done.5.refs_2_), channel_id=1, source_target_pairs={{0,1},{1,2},{2,3},{3,0},{4,5},{5,6},{6,7},{7,4},{8,9},{9,10},{10,1... | collective-permute-start | bytes 2359304 | tf_op jit(solution)/shard_map/ppermute | solution.py:130
  62.4 14.2 %collective-permute-start.11 = (bf16[2,32,1792]{2,1,0:T(8,128)(2,1)S(1)}, bf16[2,32,1792]{2,1,0:T(8,128)(2,1)S(1)}, u32[]{:S(2)}, u32[]{:S(2)}) collective-permute-start(bf16[2,32,1792]{2,1,0:T(8,128)(2,1)S(1)} %get-tuple-element.78), channel_id=1, source_target_pairs={{0,8},{8,16},{16,24},{24,0},{1,9},{9,17},{17,25},{25,1},{2,10},{10... | collective-permute-start | bytes 688136 | tf_op jit(solution)/shard_map/ppermute | solution.py:136
  64.2 13.3 %collective-permute-start.12 = (bf16[2,32,1792]{2,1,0:T(8,128)(2,1)S(1)}, bf16[2,32,1792]{2,1,0:T(8,128)(2,1)S(1)}, u32[]{:S(2)}, u32[]{:S(2)}) collective-permute-start(bf16[2,32,1792]{2,1,0:T(8,128)(2,1)S(1)} %get-tuple-element.79), channel_id=1, source_target_pairs={{0,24},{8,0},{16,8},{24,16},{1,25},{9,1},{17,9},{25,17},{2,26},{10... | collective-permute-start | bytes 688136 | tf_op jit(solution)/shard_map/ppermute | solution.py:136
  65.7 21.6 %collective-permute-start.13 = (bf16[2,32,1792]{2,1,0:T(8,128)(2,1)S(1)}, bf16[2,32,1792]{2,1,0:T(8,128)(2,1)S(1)}, u32[]{:S(2)}, u32[]{:S(2)}) collective-permute-start(bf16[2,32,1792]{2,1,0:T(8,128)(2,1)S(1)} %get-tuple-element.80), channel_id=1, source_target_pairs={{0,16},{8,24},{16,0},{24,8},{1,17},{9,25},{17,1},{25,9},{2,18},{10... | collective-permute-start | bytes 688136 | tf_op jit(solution)/shard_map/ppermute | solution.py:136
  67.8 19.5 %collective-permute-start.14 = (bf16[256,768]{1,0:T(8,128)(2,1)S(1)}, bf16[256,768]{1,0:T(8,128)(2,1)S(1)}, u32[]{:S(2)}, u32[]{:S(2)}) collective-permute-start(bf16[256,768]{1,0:T(8,128)(2,1)S(1)} %slice.44), channel_id=1, source_target_pairs={{0,4},{4,0},{1,5},{5,1},{2,6},{6,2},{3,7},{7,3},{8,12},{12,8},{9,1... | collective-permute-start | bytes 1179656 | tf_op jit(solution)/shard_map/ppermute | solution.py:133
  87.3 11.8 %collective-permute-start.15 = (bf16[2,32,1792]{2,1,0:T(8,128)(2,1)S(1)}, bf16[2,32,1792]{2,1,0:T(8,128)(2,1)S(1)}, u32[]{:S(2)}, u32[]{:S(2)}) collective-permute-start(bf16[2,32,1792]{2,1,0:T(8,128)(2,1)S(1)} %get-tuple-element.82), channel_id=1, source_target_pairs={{0,8},{8,16},{16,24},{24,0},{1,9},{9,17},{17,25},{25,1},{2,10},{10... | collective-permute-start | bytes 688136 | tf_op jit(solution)/shard_map/ppermute | solution.py:136
  88.5 11.4 %collective-permute-start.16 = (bf16[2,32,1792]{2,1,0:T(8,128)(2,1)S(1)}, bf16[2,32,1792]{2,1,0:T(8,128)(2,1)}, u32[]{:S(2)}, u32[]{:S(2)}) collective-permute-start(bf16[2,32,1792]{2,1,0:T(8,128)(2,1)S(1)} %get-tuple-element.83), channel_id=1, source_target_pairs={{0,24},{8,0},{16,8},{24,16},{1,25},{9,1},{17,9},{25,17},{2,26},{10... | collective-permute-start | bytes 688136 | tf_op jit(solution)/shard_map/ppermute | solution.py:136
  90.6 9.3 %collective-permute-start.17 = (bf16[2,32,1792]{2,1,0:T(8,128)(2,1)S(1)}, bf16[2,32,1792]{2,1,0:T(8,128)(2,1)}, u32[]{:S(2)}, u32[]{:S(2)}) collective-permute-start(bf16[2,32,1792]{2,1,0:T(8,128)(2,1)S(1)} %get-tuple-element.84), channel_id=1, source_target_pairs={{0,16},{8,24},{16,0},{24,8},{1,17},{9,25},{17,1},{25,9},{2,18},{10... | collective-permute-start | bytes 688136 | tf_op jit(solution)/shard_map/ppermute | solution.py:136
  93.1 6.8 %collective-permute-start.19 = (bf16[256,768]{1,0:T(8,128)(2,1)S(1)}, bf16[256,768]{1,0:T(8,128)(2,1)}, u32[]{:S(2)}, u32[]{:S(2)}) collective-permute-start(bf16[256,768]{1,0:T(8,128)(2,1)S(1)} %slice.47), channel_id=1, source_target_pairs={{0,4},{4,0},{1,5},{5,1},{2,6},{6,2},{3,7},{7,3},{8,12},{12,8},{9,1... | collective-permute-start | bytes 1179656 | tf_op jit(solution)/shard_map/ppermute | solution.py:133
  96.4 25.9 %collective-permute-start.23 = (bf16[32,1792]{1,0:T(8,128)(2,1)}, bf16[32,1792]{1,0:T(8,128)(2,1)S(1)}, u32[]{:S(2)}, u32[]{:S(2)}) collective-permute-start(bf16[32,1792]{1,0:T(8,128)(2,1)} %get-tuple-element.149), channel_id=1, source_target_pairs={{0,96},{32,64},{64,32},{96,0},{1,97},{33,65},{65,33},{97,1},{2,98}... | collective-permute-start | bytes 344072 | tf_op jit(solution)/shard_map/ppermute | solution.py:159
  99.2 23.1 %collective-permute-start.24 = (bf16[32,1792]{1,0:T(8,128)(2,1)}, bf16[32,1792]{1,0:T(8,128)(2,1)S(1)}, u32[]{:S(2)}, u32[]{:S(2)}) collective-permute-start(bf16[32,1792]{1,0:T(8,128)(2,1)} %get-tuple-element.148), channel_id=1, source_target_pairs={{0,64},{32,96},{64,0},{96,32},{1,65},{33,97},{65,1},{97,33},{2,66}... | collective-permute-start | bytes 344072 | tf_op jit(solution)/shard_map/ppermute | solution.py:159
  100.0 22.3 %collective-permute-start.20 = (bf16[2,32,1792]{2,1,0:T(8,128)(2,1)S(1)}, bf16[2,32,1792]{2,1,0:T(8,128)(2,1)S(1)}, u32[]{:S(2)}, u32[]{:S(2)}) collective-permute-start(bf16[2,32,1792]{2,1,0:T(8,128)(2,1)S(1)} %get-tuple-element.100), channel_id=1, source_target_pairs={{0,8},{8,16},{16,24},{24,0},{1,9},{9,17},{17,25},{25,1},{2,10},{10... | collective-permute-start | bytes 688136 | tf_op jit(solution)/shard_map/ppermute | solution.py:136
  101.3 21.1 %collective-permute-start.21 = (bf16[2,32,1792]{2,1,0:T(8,128)(2,1)S(1)}, bf16[2,32,1792]{2,1,0:T(8,128)(2,1)S(1)}, u32[]{:S(2)}, u32[]{:S(2)}) collective-permute-start(bf16[2,32,1792]{2,1,0:T(8,128)(2,1)S(1)} %get-tuple-element.101), channel_id=1, source_target_pairs={{0,24},{8,0},{16,8},{24,16},{1,25},{9,1},{17,9},{25,17},{2,26},{10... | collective-permute-start | bytes 688136 | tf_op jit(solution)/shard_map/ppermute | solution.py:136
  103.3 19.0 %collective-permute-start.22 = (bf16[2,32,1792]{2,1,0:T(8,128)(2,1)S(1)}, bf16[2,32,1792]{2,1,0:T(8,128)(2,1)S(1)}, u32[]{:S(2)}, u32[]{:S(2)}) collective-permute-start(bf16[2,32,1792]{2,1,0:T(8,128)(2,1)S(1)} %get-tuple-element.102), channel_id=1, source_target_pairs={{0,16},{8,24},{16,0},{24,8},{1,17},{9,25},{17,1},{25,9},{2,18},{10... | collective-permute-start | bytes 688136 | tf_op jit(solution)/shard_map/ppermute | solution.py:136
  132.5 8.9 %collective-permute-start.28 = (bf16[32,1792]{1,0:T(8,128)(2,1)S(1)}, bf16[32,1792]{1,0:T(8,128)(2,1)S(1)}, u32[]{:S(2)}, u32[]{:S(2)}) collective-permute-start(bf16[32,1792]{1,0:T(8,128)(2,1)S(1)} %get-tuple-element.131), channel_id=1, source_target_pairs={{0,128},{128,0},{1,129},{129,1},{2,130},{130,2},{3,131},{131,3},{4... | collective-permute-start | bytes 344072 | tf_op jit(solution)/shard_map/ppermute | solution.py:210
  (18 other events, 122.6 us)
Sparse Core Ops, SparseCore 0:
  22.3 67.1 all-gather.1

commit v4 on v3

--- a/solution.py
+++ b/solution.py
@@ -185,22 +185,22 @@
     slot3, y1, other2, p2, slot2 = bar((slot3, y1, other2, p2, slot2))
 
     y0, y1 = bar((summed(p0[0], y0), summed(p1[0], y1)))
-    y2 = over_y(*p2[1:])
     x01 = over_x((1,), at_x(y0, y1))
     other3 = for_grads(slot3)
     p3 = products(slot3)
-    y2, x01, p3, slot3, other3, whole, tt, cc = bar((y2, x01, p3, slot3, other3, whole, t, c))
+    sent = [jnp.concatenate(blocks) for blocks in zip(p2[1:], p3[1:])]
+    x01, sent, p3, slot3, other3, whole, tt, cc = bar((x01, sent, p3[0], slot3, other3, whole, t, c))
 
     places = jnp.stack([(tt - k) % 4 for k in range(4)] + [cc, 1 - cc]).astype(jnp.int32)
     slots = (slot0, slot1, slot2, slot3)
     others = (other0, other1, other2, other3)
-    y3 = over_y(*p3[1:])
+    y23 = over_y(*sent)
     x01 += over_x((3, 2), at_x(y0, y1))
     grads = grads_of(places, slots, others, whole.reshape(4, 8, 2, 32, cols), codes)
-    y2 = summed(p2[0], y2)
-    y2, y3, x01, grads = bar((y2, y3, x01, grads))
-
-    y3 = summed(p3[0], y3)
+    y23, x01, grads = bar((y23, x01, grads))
+
+    y2 = summed(p2[0], [block[:2] for block in y23])
+    y3 = summed(p3, [block[2:] for block in y23])
     x23 = over_x((1, 3, 2), at_x(y2, y3))
     first = summed(at_x(y0, y1)(0), x01)
     x23, first = bar((x23, first))

time: 149 us -> 147 us (0.987)
  starting transfers between devices: 44.8 us -> 38.9 us
  waiting for transfers between devices: 55 us -> 57.4 us
    ppermute x12 -> x9, starting transfers between devices: 19.7 us -> 14.1 us  [over_y(): lax.ppermute(b, 'y', shift(4, d))]
    ppermute x12 -> x9, waiting for transfers between devices: 24.5 us -> 29.1 us  [over_y(): lax.ppermute(b, 'y', shift(4, d))]
    ppermute x6, waiting for transfers between devices: 6.88 us -> 4.18 us  [over_x(): return [lax.ppermute(rows(m).astype(BF), 'x', flip(4, m)) for m in places]]
  transfers between devices with their start and end apart: 30 -> 27, of which waited for: 15 -> 15; matrix products, arithmetic and copies ran while one was open for 8% -> 8% of each run, Pallas kernels for 13% -> 13%
where the time goes in v4:
time: 147 us; the launch traced here: 146 us
  waiting for transfers between devices  57.4 us (39%)
  starting transfers between devices  38.9 us (26%)
  Pallas kernels  19.7 us (13%)
  between operations  14.7 us (10%)
  matrix products  7.08 us (5%)
  other arithmetic  5.06 us (3%)
  local copies, waits for them, and re-layouts  3.47 us (2%)
    ppermute x9, waiting for transfers between devices, over_y(): lax.ppermute(b, 'y', shift(4, d))  29.1 us
    ppermute x3, waiting for transfers between devices, ring(): return lax.ppermute(slot, 't', shift(4, 1))  15.1 us
    pallas_call x1, Pallas kernels, grads_of(): pl.pallas_call(grads_kernel, grid_spec=pltpu.PrefetchScalarGridSpec(num_s...  14.9 us
    ppermute x9, starting transfers between devices, over_y(): lax.ppermute(b, 'y', shift(4, d))  14.1 us
    ppermute x6, starting transfers between devices, over_x(): return [lax.ppermute(rows(m).astype(BF), 'x', flip(4, m)) for m in places]  8.61 us
    ppermute x1, starting transfers between devices, on_device(): peer = lax.ppermute(after(weight, sent), 'zh', shift(2, 1))  6.38 us
    ppermute x1, starting transfers between devices, on_device(): lax.ppermute(jnp.where(here, second, first).astype(BF), 'zh', shift(2, 1))  5.35 us
    pallas_call x1, Pallas kernels, hidden_of(): pl.pallas_call(hidden_kernel, grid=(2,), in_specs=[rows, rows, scale, sca...  4.8 us
  transfers between devices with their start and end apart: 27, of which 15 were waited for; matrix products, arithmetic and copies ran while one was open for 8% of the time, Pallas kernels for 13%

profile of v4, /device:TPU:32, one launch (start us, length us, event | category | flops | bytes accessed | tf_op | source)
XLA Modules:
  0.0 146.3 jit_solution(2658904380537397867)
XLA Ops:
  7.2 1.4 copy.22
  8.8 6.4 %collective-permute-start.1 = (bf16[32,1792]{1,0:T(8,128)(2,1)S(1)}, bf16[32,1792]{1,0:T(8,128)(2,1)S(1)}, u32[]{:S(2)}, u32[]{:S(2)}) collective-permute-start(bf16[32,1792]{1,0:T(8,128)(2,1)S(1)} %copy-done.8), channel_id=1, source_target_pairs={{0,128},{128,0},{1,129},{129,1},{2,130},{130,2},{3,131},{131,3},{4... | collective-permute-start | bytes 344072 | tf_op jit(solution)/shard_map/ppermute | solution.py:163
  15.2 4.8 %shard_map.85 = bf16[768,1792]{1,0:T(8,128)(2,1)} custom-call(bf16[768,1792]{1,0:T(8,128)(2,1)} %refs_9_.1, bf16[768,1792]{1,0:T(8,128)(2,1)} %refs_10_.1, f32[768]{0:T(1024)} %refs_11_.1, f32[768]{0:T(1024)} %refs_12_.1), custom_call_target="tpu_custom_call" | custom-call | flops 49999998976 | tf_op jit(solution)/shard_map/pallas_call | solution.py:52
  24.0 3.5 %collective-permute-done.3 = bf16[768,1792]{1,0:T(8,128)(2,1)S(1)} collective-permute-done((bf16[768,1792]{1,0:T(8,128)(2,1)}, bf16[768,1792]{1,0:T(8,128)(2,1)S(1)}, u32[]{:S(2)}, u32[]{:S(2)}) %collective-permute-start.3) | collective-permute-done | bytes 2752544 | tf_op jit(solution)/shard_map/ppermute | solution.py:133
  29.5 12.7 %collective-permute-done.2.refs_1_ = bf16[256,1536]{1,0:T(8,128)(2,1)S(1)} collective-permute-done((bf16[256,1536]{1,0:T(8,128)(2,1)S(1)}, bf16[256,1536]{1,0:T(8,128)(2,1)S(1)}, u32[]{:S(2)}, u32[]{:S(2)}) %collective-permute-start.2) | collective-permute-done | bytes 786464 | tf_op jit(solution)/shard_map/ppermute | solution.py:130
  43.5 1.7 %collective-permute-start.6 = (bf16[2,32,1792]{2,1,0:T(8,128)(2,1)S(1)}, bf16[2,32,1792]{2,1,0:T(8,128)(2,1)S(1)}, u32[]{:S(2)}, u32[]{:S(2)}) collective-permute-start(bf16[2,32,1792]{2,1,0:T(8,128)(2,1)S(1)} %get-tuple-element.70), channel_id=1, source_target_pairs={{0,8},{8,16},{16,24},{24,0},{1,9},{9,17},{17,25},{25,1},{2,10},{10... | collective-permute-start | bytes 688136 | tf_op jit(solution)/shard_map/ppermute | solution.py:136
  45.3 1.6 %collective-permute-start.7 = (bf16[2,32,1792]{2,1,0:T(8,128)(2,1)S(1)}, bf16[2,32,1792]{2,1,0:T(8,128)(2,1)S(1)}, u32[]{:S(2)}, u32[]{:S(2)}) collective-permute-start(bf16[2,32,1792]{2,1,0:T(8,128)(2,1)S(1)} %get-tuple-element.71), channel_id=1, source_target_pairs={{0,24},{8,0},{16,8},{24,16},{1,25},{9,1},{17,9},{25,17},{2,26},{10... | collective-permute-start | bytes 688136 | tf_op jit(solution)/shard_map/ppermute | solution.py:136
  46.9 2.1 %collective-permute-start.8 = (bf16[2,32,1792]{2,1,0:T(8,128)(2,1)S(1)}, bf16[2,32,1792]{2,1,0:T(8,128)(2,1)S(1)}, u32[]{:S(2)}, u32[]{:S(2)}) collective-permute-start(bf16[2,32,1792]{2,1,0:T(8,128)(2,1)S(1)} %get-tuple-element.72), channel_id=1, source_target_pairs={{0,16},{8,24},{16,0},{24,8},{1,17},{9,25},{17,1},{25,9},{2,18},{10... | collective-permute-start | bytes 688136 | tf_op jit(solution)/shard_map/ppermute | solution.py:136
  50.9 1.8 %collective-permute-done.6 = bf16[2,32,1792]{2,1,0:T(8,128)(2,1)S(1)} collective-permute-done((bf16[2,32,1792]{2,1,0:T(8,128)(2,1)S(1)}, bf16[2,32,1792]{2,1,0:T(8,128)(2,1)S(1)}, u32[]{:S(2)}, u32[]{:S(2)}) %collective-permute-start.6) | collective-permute-done | bytes 229408 | tf_op jit(solution)/shard_map/ppermute | solution.py:136
  53.7 4.9 %collective-permute-done.8 = bf16[2,32,1792]{2,1,0:T(8,128)(2,1)S(1)} collective-permute-done((bf16[2,32,1792]{2,1,0:T(8,128)(2,1)S(1)}, bf16[2,32,1792]{2,1,0:T(8,128)(2,1)S(1)}, u32[]{:S(2)}, u32[]{:S(2)}) %collective-permute-start.8) | collective-permute-done | bytes 229408 | tf_op jit(solution)/shard_map/ppermute | solution.py:136
  58.7 2.4 %collective-permute-done.5.refs_2_ = bf16[256,1536]{1,0:T(8,128)(2,1)S(1)} collective-permute-done((bf16[256,1536]{1,0:T(8,128)(2,1)S(1)}, bf16[256,1536]{1,0:T(8,128)(2,1)S(1)}, u32[]{:S(2)}, u32[]{:S(2)}) %collective-permute-start.5) | collective-permute-done | bytes 786464 | tf_op jit(solution)/shard_map/ppermute | solution.py:130
  62.4 1.7 %collective-permute-start.11 = (bf16[2,32,1792]{2,1,0:T(8,128)(2,1)S(1)}, bf16[2,32,1792]{2,1,0:T(8,128)(2,1)S(1)}, u32[]{:S(2)}, u32[]{:S(2)}) collective-permute-start(bf16[2,32,1792]{2,1,0:T(8,128)(2,1)S(1)} %get-tuple-element.79), channel_id=1, source_target_pairs={{0,8},{8,16},{16,24},{24,0},{1,9},{9,17},{17,25},{25,1},{2,10},{10... | collective-permute-start | bytes 688136 | tf_op jit(solution)/shard_map/ppermute | solution.py:136
  64.2 1.6 %collective-permute-start.12 = (bf16[2,32,1792]{2,1,0:T(8,128)(2,1)S(1)}, bf16[2,32,1792]{2,1,0:T(8,128)(2,1)S(1)}, u32[]{:S(2)}, u32[]{:S(2)}) collective-permute-start(bf16[2,32,1792]{2,1,0:T(8,128)(2,1)S(1)} %get-tuple-element.80), channel_id=1, source_target_pairs={{0,24},{8,0},{16,8},{24,16},{1,25},{9,1},{17,9},{25,17},{2,26},{10... | collective-permute-start | bytes 688136 | tf_op jit(solution)/shard_map/ppermute | solution.py:136
  65.7 2.1 %collective-permute-start.13 = (bf16[2,32,1792]{2,1,0:T(8,128)(2,1)S(1)}, bf16[2,32,1792]{2,1,0:T(8,128)(2,1)S(1)}, u32[]{:S(2)}, u32[]{:S(2)}) collective-permute-start(bf16[2,32,1792]{2,1,0:T(8,128)(2,1)S(1)} %get-tuple-element.81), channel_id=1, source_target_pairs={{0,16},{8,24},{16,0},{24,8},{1,17},{9,25},{17,1},{25,9},{2,18},{10... | collective-permute-start | bytes 688136 | tf_op jit(solution)/shard_map/ppermute | solution.py:136
  70.6 6.0 %collective-permute-done.11 = bf16[2,32,1792]{2,1,0:T(8,128)(2,1)S(1)} collective-permute-done((bf16[2,32,1792]{2,1,0:T(8,128)(2,1)S(1)}, bf16[2,32,1792]{2,1,0:T(8,128)(2,1)S(1)}, u32[]{:S(2)}, u32[]{:S(2)}) %collective-permute-start.11) | collective-permute-done | bytes 229408 | tf_op jit(solution)/shard_map/ppermute | solution.py:136
  77.5 9.8 %collective-permute-done.13 = bf16[2,32,1792]{2,1,0:T(8,128)(2,1)S(1)} collective-permute-done((bf16[2,32,1792]{2,1,0:T(8,128)(2,1)S(1)}, bf16[2,32,1792]{2,1,0:T(8,128)(2,1)S(1)}, u32[]{:S(2)}, u32[]{:S(2)}) %collective-permute-start.13) | collective-permute-done | bytes 229408 | tf_op jit(solution)/shard_map/ppermute | solution.py:136
  89.9 2.2 %collective-permute-start.20 = (bf16[32,1792]{1,0:T(8,128)(2,1)}, bf16[32,1792]{1,0:T(8,128)(2,1)}, u32[]{:S(2)}, u32[]{:S(2)}) collective-permute-start(bf16[32,1792]{1,0:T(8,128)(2,1)} %get-tuple-element.143), channel_id=1, source_target_pairs={{0,96},{32,64},{64,32},{96,0},{1,97},{33,65},{65,33},{97,1},{2,98}... | collective-permute-start | bytes 344072 | tf_op jit(solution)/shard_map/ppermute | solution.py:159
  97.1 2.2 %collective-permute-start.18 = (bf16[4,32,1792]{2,1,0:T(8,128)(2,1)S(1)}, bf16[4,32,1792]{2,1,0:T(8,128)(2,1)S(1)}, u32[]{:S(2)}, u32[]{:S(2)}) collective-permute-start(bf16[4,32,1792]{2,1,0:T(8,128)(2,1)S(1)} %get-tuple-element.93), channel_id=1, source_target_pairs={{0,24},{8,0},{16,8},{24,16},{1,25},{9,1},{17,9},{25,17},{2,26},{10... | collective-permute-start | bytes 1376264 | tf_op jit(solution)/shard_map/ppermute | solution.py:136
  99.9 14.9 %shard_map.86 = (bf16[768,1792]{1,0:T(8,128)(2,1)}, bf16[768,1792]{1,0:T(8,128)(2,1)}) custom-call(s32[6]{0:T(128)} %stack.45.places, bf16[256,1536]{1,0:T(8,128)(2,1)} %copy-done.1, bf16[256,1536]{1,0:T(8,128)(2,1)} %copy-done.5, bf16[256,1536]{1,0:T(8,128)(2,1)} %copy-done.6, bf16[256,1536]{1,0:T(8,128)(2,1)} %copy-done.7, bf16[256,768]{1,0:T(8,128)(2,1)} %copy-done.9, ...), custom_call_target="tpu_custom_call" | custom-call | flops 49999998976 | tf_op jit(solution)/shard_map/pallas_call | solution.py:96
  114.8 4.6 %collective-permute-done.17 = bf16[4,32,1792]{2,1,0:T(8,128)(2,1)S(1)} collective-permute-done((bf16[4,32,1792]{2,1,0:T(8,128)(2,1)S(1)}, bf16[4,32,1792]{2,1,0:T(8,128)(2,1)S(1)}, u32[]{:S(2)}, u32[]{:S(2)}) %collective-permute-start.17) | collective-permute-done | bytes 458784 | tf_op jit(solution)/shard_map/ppermute | solution.py:136
  120.8 2.1 %collective-permute-start.23 = (bf16[32,1792]{1,0:T(8,128)(2,1)S(1)}, bf16[32,1792]{1,0:T(8,128)(2,1)S(1)}, u32[]{:S(2)}, u32[]{:S(2)}) collective-permute-start(bf16[32,1792]{1,0:T(8,128)(2,1)S(1)} %get-tuple-element.140), channel_id=1, source_target_pairs={{0,96},{32,64},{64,32},{96,0},{1,97},{33,65},{65,33},{97,1},{2,98}... | collective-permute-start | bytes 344072 | tf_op jit(solution)/shard_map/ppermute | solution.py:159
  125.6 2.4 %collective-permute-done.23 = bf16[32,1792]{1,0:T(8,128)(2,1)S(1)} collective-permute-done((bf16[32,1792]{1,0:T(8,128)(2,1)S(1)}, bf16[32,1792]{1,0:T(8,128)(2,1)S(1)}, u32[]{:S(2)}, u32[]{:S(2)}) %collective-permute-start.23) | collective-permute-done | bytes 114720 | tf_op jit(solution)/shard_map/ppermute | solution.py:159
  129.3 5.4 %collective-permute-start.25 = (bf16[32,1792]{1,0:T(8,128)(2,1)S(1)}, bf16[32,1792]{1,0:T(8,128)(2,1)S(1)}, u32[]{:S(2)}, u32[]{:S(2)}) collective-permute-start(bf16[32,1792]{1,0:T(8,128)(2,1)S(1)} %get-tuple-element.123), channel_id=1, source_target_pairs={{0,128},{128,0},{1,129},{129,1},{2,130},{130,2},{3,131},{131,3},{4... | collective-permute-start | bytes 344072 | tf_op jit(solution)/shard_map/ppermute | solution.py:210
  134.6 4.1 %collective-permute-done.25 = bf16[32,1792]{1,0:T(8,128)(2,1)S(1)} collective-permute-done((bf16[32,1792]{1,0:T(8,128)(2,1)S(1)}, bf16[32,1792]{1,0:T(8,128)(2,1)S(1)}, u32[]{:S(2)}, u32[]{:S(2)}) %collective-permute-start.25) | collective-permute-done | bytes 114720 | tf_op jit(solution)/shard_map/ppermute | solution.py:210
  (92 shorter events, 29.3 us)
Async XLA Ops:
  7.2 88.7 %all-gather.2.cloned.1.call-start = ((), (), s32[]{:S(2)}) async-start(), calls=%async_computation | async-start | bytes 7569408 | tf_op jit(solution)/shard_map/all_gather | solution.py:167
  8.7 11.3 %collective-permute-start = (bf16[256,768]{1,0:T(8,128)(2,1)S(1)}, bf16[256,768]{1,0:T(8,128)(2,1)S(1)}, u32[]{:S(2)}, u32[]{:S(2)}) collective-permute-start(bf16[256,768]{1,0:T(8,128)(2,1)S(1)} %bitcast.143), channel_id=1, source_target_pairs={{0,4},{4,0},{1,5},{5,1},{2,6},{6,2},{3,7},{7,3},{8,12},{12,8},{9,1... | collective-permute-start | bytes 1179656 | tf_op jit(solution)/shard_map/ppermute | solution.py:133
  8.8 12.6 %collective-permute-start.1 = (bf16[32,1792]{1,0:T(8,128)(2,1)S(1)}, bf16[32,1792]{1,0:T(8,128)(2,1)S(1)}, u32[]{:S(2)}, u32[]{:S(2)}) collective-permute-start(bf16[32,1792]{1,0:T(8,128)(2,1)S(1)} %copy-done.8), channel_id=1, source_target_pairs={{0,128},{128,0},{1,129},{129,1},{2,130},{130,2},{3,131},{131,3},{4... | collective-permute-start | bytes 344072 | tf_op jit(solution)/shard_map/ppermute | solution.py:163
  22.5 19.7 %collective-permute-start.2 = (bf16[256,1536]{1,0:T(8,128)(2,1)S(1)}, bf16[256,1536]{1,0:T(8,128)(2,1)S(1)}, u32[]{:S(2)}, u32[]{:S(2)}) collective-permute-start(bf16[256,1536]{1,0:T(8,128)(2,1)S(1)} %pad_maximum_fusion.refs_0_), channel_id=1, source_target_pairs={{0,1},{1,2},{2,3},{3,0},{4,5},{5,6},{6,7},{7,4},{8,9},{9,10},{10,1... | collective-permute-start | bytes 2359304 | tf_op jit(solution)/shard_map/ppermute | solution.py:130
  42.2 18.9 %collective-permute-start.5 = (bf16[256,1536]{1,0:T(8,128)(2,1)S(1)}, bf16[256,1536]{1,0:T(8,128)(2,1)S(1)}, u32[]{:S(2)}, u32[]{:S(2)}) collective-permute-start(bf16[256,1536]{1,0:T(8,128)(2,1)S(1)} %collective-permute-done.2.refs_1_), channel_id=1, source_target_pairs={{0,1},{1,2},{2,3},{3,0},{4,5},{5,6},{6,7},{7,4},{8,9},{9,10},{10,1... | collective-permute-start | bytes 2359304 | tf_op jit(solution)/shard_map/ppermute | solution.py:130
  43.5 9.1 %collective-permute-start.6 = (bf16[2,32,1792]{2,1,0:T(8,128)(2,1)S(1)}, bf16[2,32,1792]{2,1,0:T(8,128)(2,1)S(1)}, u32[]{:S(2)}, u32[]{:S(2)}) collective-permute-start(bf16[2,32,1792]{2,1,0:T(8,128)(2,1)S(1)} %get-tuple-element.70), channel_id=1, source_target_pairs={{0,8},{8,16},{16,24},{24,0},{1,9},{9,17},{17,25},{25,1},{2,10},{10... | collective-permute-start | bytes 688136 | tf_op jit(solution)/shard_map/ppermute | solution.py:136
  45.3 8.4 %collective-permute-start.7 = (bf16[2,32,1792]{2,1,0:T(8,128)(2,1)S(1)}, bf16[2,32,1792]{2,1,0:T(8,128)(2,1)S(1)}, u32[]{:S(2)}, u32[]{:S(2)}) collective-permute-start(bf16[2,32,1792]{2,1,0:T(8,128)(2,1)S(1)} %get-tuple-element.71), channel_id=1, source_target_pairs={{0,24},{8,0},{16,8},{24,16},{1,25},{9,1},{17,9},{25,17},{2,26},{10... | collective-permute-start | bytes 688136 | tf_op jit(solution)/shard_map/ppermute | solution.py:136
  46.9 11.8 %collective-permute-start.8 = (bf16[2,32,1792]{2,1,0:T(8,128)(2,1)S(1)}, bf16[2,32,1792]{2,1,0:T(8,128)(2,1)S(1)}, u32[]{:S(2)}, u32[]{:S(2)}) collective-permute-start(bf16[2,32,1792]{2,1,0:T(8,128)(2,1)S(1)} %get-tuple-element.72), channel_id=1, source_target_pairs={{0,16},{8,24},{16,0},{24,8},{1,17},{9,25},{17,1},{25,9},{2,18},{10... | collective-permute-start | bytes 688136 | tf_op jit(solution)/shard_map/ppermute | solution.py:136
  48.9 9.7 %collective-permute-start.9 = (bf16[256,768]{1,0:T(8,128)(2,1)S(1)}, bf16[256,768]{1,0:T(8,128)(2,1)S(1)}, u32[]{:S(2)}, u32[]{:S(2)}) collective-permute-start(bf16[256,768]{1,0:T(8,128)(2,1)S(1)} %slice.60), channel_id=1, source_target_pairs={{0,4},{4,0},{1,5},{5,1},{2,6},{6,2},{3,7},{7,3},{8,12},{12,8},{9,1... | collective-permute-start | bytes 1179656 | tf_op jit(solution)/shard_map/ppermute | solution.py:133
  61.1 26.2 %collective-permute-start.10 = (bf16[256,1536]{1,0:T(8,128)(2,1)S(1)}, bf16[256,1536]{1,0:T(8,128)(2,1)S(1)}, u32[]{:S(2)}, u32[]{:S(2)}) collective-permute-start(bf16[256,1536]{1,0:T(8,128)(2,1)S(1)} %collective-permute-done.5.refs_2_), channel_id=1, source_target_pairs={{0,1},{1,2},{2,3},{3,0},{4,5},{5,6},{6,7},{7,4},{8,9},{9,10},{10,1... | collective-permute-start | bytes 2359304 | tf_op jit(solution)/shard_map/ppermute | solution.py:130
  62.4 14.2 %collective-permute-start.11 = (bf16[2,32,1792]{2,1,0:T(8,128)(2,1)S(1)}, bf16[2,32,1792]{2,1,0:T(8,128)(2,1)S(1)}, u32[]{:S(2)}, u32[]{:S(2)}) collective-permute-start(bf16[2,32,1792]{2,1,0:T(8,128)(2,1)S(1)} %get-tuple-element.79), channel_id=1, source_target_pairs={{0,8},{8,16},{16,24},{24,0},{1,9},{9,17},{17,25},{25,1},{2,10},{10... | collective-permute-start | bytes 688136 | tf_op jit(solution)/shard_map/ppermute | solution.py:136
  64.2 13.3 %collective-permute-start.12 = (bf16[2,32,1792]{2,1,0:T(8,128)(2,1)S(1)}, bf16[2,32,1792]{2,1,0:T(8,128)(2,1)S(1)}, u32[]{:S(2)}, u32[]{:S(2)}) collective-permute-start(bf16[2,32,1792]{2,1,0:T(8,128)(2,1)S(1)} %get-tuple-element.80), channel_id=1, source_target_pairs={{0,24},{8,0},{16,8},{24,16},{1,25},{9,1},{17,9},{25,17},{2,26},{10... | collective-permute-start | bytes 688136 | tf_op jit(solution)/shard_map/ppermute | solution.py:136
  65.7 21.6 %collective-permute-start.13 = (bf16[2,32,1792]{2,1,0:T(8,128)(2,1)S(1)}, bf16[2,32,1792]{2,1,0:T(8,128)(2,1)S(1)}, u32[]{:S(2)}, u32[]{:S(2)}) collective-permute-start(bf16[2,32,1792]{2,1,0:T(8,128)(2,1)S(1)} %get-tuple-element.81), channel_id=1, source_target_pairs={{0,16},{8,24},{16,0},{24,8},{1,17},{9,25},{17,1},{25,9},{2,18},{10... | collective-permute-start | bytes 688136 | tf_op jit(solution)/shard_map/ppermute | solution.py:136
  67.8 19.5 %collective-permute-start.14 = (bf16[256,768]{1,0:T(8,128)(2,1)S(1)}, bf16[256,768]{1,0:T(8,128)(2,1)S(1)}, u32[]{:S(2)}, u32[]{:S(2)}) collective-permute-start(bf16[256,768]{1,0:T(8,128)(2,1)S(1)} %slice.62), channel_id=1, source_target_pairs={{0,4},{4,0},{1,5},{5,1},{2,6},{6,2},{3,7},{7,3},{8,12},{12,8},{9,1... | collective-permute-start | bytes 1179656 | tf_op jit(solution)/shard_map/ppermute | solution.py:133
  88.4 7.4 %collective-permute-start.15 = (bf16[32,1792]{1,0:T(8,128)(2,1)S(1)}, bf16[32,1792]{1,0:T(8,128)(2,1)}, u32[]{:S(2)}, u32[]{:S(2)}) collective-permute-start(bf16[32,1792]{1,0:T(8,128)(2,1)S(1)} %get-tuple-element.144), channel_id=1, source_target_pairs={{0,32},{32,0},{64,96},{96,64},{1,33},{33,1},{65,97},{97,65},{2,34}... | collective-permute-start | bytes 344072 | tf_op jit(solution)/shard_map/ppermute | solution.py:159
  89.8 6.0 %collective-permute-start.16 = (bf16[256,768]{1,0:T(8,128)(2,1)S(1)}, bf16[256,768]{1,0:T(8,128)(2,1)}, u32[]{:S(2)}, u32[]{:S(2)}) collective-permute-start(bf16[256,768]{1,0:T(8,128)(2,1)S(1)} %slice.65), channel_id=1, source_target_pairs={{0,4},{4,0},{1,5},{5,1},{2,6},{6,2},{3,7},{7,3},{8,12},{12,8},{9,1... | collective-permute-start | bytes 1179656 | tf_op jit(solution)/shard_map/ppermute | solution.py:133
  89.9 24.9 %collective-permute-start.20 = (bf16[32,1792]{1,0:T(8,128)(2,1)}, bf16[32,1792]{1,0:T(8,128)(2,1)}, u32[]{:S(2)}, u32[]{:S(2)}) collective-permute-start(bf16[32,1792]{1,0:T(8,128)(2,1)} %get-tuple-element.143), channel_id=1, source_target_pairs={{0,96},{32,64},{64,32},{96,0},{1,97},{33,65},{65,33},{97,1},{2,98}... | collective-permute-start | bytes 344072 | tf_op jit(solution)/shard_map/ppermute | solution.py:159
  92.1 22.7 %collective-permute-start.21 = (bf16[32,1792]{1,0:T(8,128)(2,1)}, bf16[32,1792]{1,0:T(8,128)(2,1)}, u32[]{:S(2)}, u32[]{:S(2)}) collective-permute-start(bf16[32,1792]{1,0:T(8,128)(2,1)} %get-tuple-element.142), channel_id=1, source_target_pairs={{0,64},{32,96},{64,0},{96,32},{1,65},{33,97},{65,1},{97,33},{2,66}... | collective-permute-start | bytes 344072 | tf_op jit(solution)/shard_map/ppermute | solution.py:159
  95.9 23.6 %collective-permute-start.17 = (bf16[4,32,1792]{2,1,0:T(8,128)(2,1)S(1)}, bf16[4,32,1792]{2,1,0:T(8,128)(2,1)S(1)}, u32[]{:S(2)}, u32[]{:S(2)}) collective-permute-start(bf16[4,32,1792]{2,1,0:T(8,128)(2,1)S(1)} %get-tuple-element.92), channel_id=1, source_target_pairs={{0,8},{8,16},{16,24},{24,0},{1,9},{9,17},{17,25},{25,1},{2,10},{10... | collective-permute-start | bytes 1376264 | tf_op jit(solution)/shard_map/ppermute | solution.py:136
  97.1 22.4 %collective-permute-start.18 = (bf16[4,32,1792]{2,1,0:T(8,128)(2,1)S(1)}, bf16[4,32,1792]{2,1,0:T(8,128)(2,1)S(1)}, u32[]{:S(2)}, u32[]{:S(2)}) collective-permute-start(bf16[4,32,1792]{2,1,0:T(8,128)(2,1)S(1)} %get-tuple-element.93), channel_id=1, source_target_pairs={{0,24},{8,0},{16,8},{24,16},{1,25},{9,1},{17,9},{25,17},{2,26},{10... | collective-permute-start | bytes 1376264 | tf_op jit(solution)/shard_map/ppermute | solution.py:136
  99.2 20.3 %collective-permute-start.19 = (bf16[4,32,1792]{2,1,0:T(8,128)(2,1)}, bf16[4,32,1792]{2,1,0:T(8,128)(2,1)S(1)}, u32[]{:S(2)}, u32[]{:S(2)}) collective-permute-start(bf16[4,32,1792]{2,1,0:T(8,128)(2,1)} %pad_maximum_fusion.3), channel_id=1, source_target_pairs={{0,16},{8,24},{16,0},{24,8},{1,17},{9,25},{17,1},{25,9},{2,18},{10... | collective-permute-start | bytes 1376264 | tf_op jit(solution)/shard_map/ppermute | solution.py:136
  120.8 7.1 %collective-permute-start.23 = (bf16[32,1792]{1,0:T(8,128)(2,1)S(1)}, bf16[32,1792]{1,0:T(8,128)(2,1)S(1)}, u32[]{:S(2)}, u32[]{:S(2)}) collective-permute-start(bf16[32,1792]{1,0:T(8,128)(2,1)S(1)} %get-tuple-element.140), channel_id=1, source_target_pairs={{0,96},{32,64},{64,32},{96,0},{1,97},{33,65},{65,33},{97,1},{2,98}... | collective-permute-start | bytes 344072 | tf_op jit(solution)/shard_map/ppermute | solution.py:159
  122.9 6.3 %collective-permute-start.24 = (bf16[32,1792]{1,0:T(8,128)(2,1)S(1)}, bf16[32,1792]{1,0:T(8,128)(2,1)S(1)}, u32[]{:S(2)}, u32[]{:S(2)}) collective-permute-start(bf16[32,1792]{1,0:T(8,128)(2,1)S(1)} %get-tuple-element.139), channel_id=1, source_target_pairs={{0,64},{32,96},{64,0},{96,32},{1,65},{33,97},{65,1},{97,33},{2,66}... | collective-permute-start | bytes 344072 | tf_op jit(solution)/shard_map/ppermute | solution.py:159
  129.3 9.5 %collective-permute-start.25 = (bf16[32,1792]{1,0:T(8,128)(2,1)S(1)}, bf16[32,1792]{1,0:T(8,128)(2,1)S(1)}, u32[]{:S(2)}, u32[]{:S(2)}) collective-permute-start(bf16[32,1792]{1,0:T(8,128)(2,1)S(1)} %get-tuple-element.123), channel_id=1, source_target_pairs={{0,128},{128,0},{1,129},{129,1},{2,130},{130,2},{3,131},{131,3},{4... | collective-permute-start | bytes 344072 | tf_op jit(solution)/shard_map/ppermute | solution.py:210
  (15 other events, 111.3 us)
Sparse Core Ops, SparseCore 0:
  22.3 67.1 all-gather.1
